TPU v7x, 32 devices: a whole 2x2x4 slice. The times are simulated.
32 devices in a mesh: sta: 8 (over y, x, core), tm: 4 (over z).
Axes of the slice: x: 2, y: 2, z: 4, core: 2. Of those that a mesh axis runs over, the one named last changes fastest.
Arguments:
- spectra: bfloat16 [8, 1024, 2, 4096], P('tm', None, None, 'sta')
- src_ids: int32 [3, 8], replicated, may hold values from 0 to 1023, as said below
Outputs:
- correlations: float32 [3, 256, 8, 1024], P(None, 'tm', None, 'sta')
Inputs may be any that keep to these rules, and one draw needn't show every extreme that they name: `src_ids`: the 8 ids of a round are distinct and all lie in one block of 128 consecutive stations that starts at a multiple of 128.
All inputs are finite; a program needn't handle non-finite values.
Results may differ from a plain program's by a relative error of at most 0.0056.
Values may be sent and summed in bfloat16 or wider, within the bound.
A program may use at most 128 MiB of HBM per device.

v0:
```python
import math

import jax
import jax.numpy as jnp
from jax import lax
from jax.sharding import PartitionSpec as P

BINS = 4096
BLOCK = 64
LAGS = 256
NSRC = 8
ROUNDS = 3


EPSILON = 1e-05


def spread(value, axis, root):
    mine = lax.axis_index(axis) == root
    return lax.psum(jnp.where(mine, value, jnp.zeros_like(value)), axis)


def block_sums(spec):
    values = spec.astype(jnp.float32)
    magnitude = jnp.sqrt(
        values[..., 0, :] * values[..., 0, :] + values[..., 1, :] * values[..., 1, :]
    )
    full_shape = magnitude.shape
    return magnitude.reshape(full_shape[:-1] + (full_shape[-1] // BLOCK, BLOCK)).sum(axis=-1)


def level_divide(spec, padded):
    block_num = padded.shape[-1] - 2
    level_mean = (padded[..., :-2] + padded[..., 1:-1] + padded[..., 2:]) / (3.0 * BLOCK)
    full_shape = spec.shape
    grid_view = spec.astype(jnp.float32).reshape(full_shape[:-1] + (block_num, BLOCK))
    whitened = grid_view / (level_mean[..., None, :, None] + EPSILON)
    return whitened.reshape(full_shape).astype(jnp.bfloat16)


def make_table(total_hours):
    lag_index = lax.iota(jnp.int32, LAGS) - LAGS // 2
    freq_index = lax.iota(jnp.int32, BINS)
    phase_int = jnp.remainder(lag_index[:, None] * freq_index[None, :], 2 * BINS)
    angle_rad = 2.0 * math.pi / (2 * BINS) * phase_int.astype(jnp.float32)
    norm_scale = 1.0 / math.sqrt(BINS * total_hours)
    return jnp.concatenate(
        [jnp.cos(angle_rad) * norm_scale, -jnp.sin(angle_rad) * norm_scale], axis=1
    ).astype(jnp.bfloat16)


def cross_block(sources, receivers):
    source_f = sources.astype(jnp.float32)
    receive_f = receivers.astype(jnp.float32)
    real_part = jnp.sum(
        source_f[:, :, None, 0] * receive_f[:, None, :, 0]
        + source_f[:, :, None, 1] * receive_f[:, None, :, 1],
        axis=0,
    )
    imag_part = jnp.sum(
        source_f[:, :, None, 1] * receive_f[:, None, :, 0]
        - source_f[:, :, None, 0] * receive_f[:, None, :, 1],
        axis=0,
    )
    count_src = sources.shape[1]
    count_rcv = receivers.shape[1]
    stacked = jnp.stack([real_part, imag_part], axis=2).astype(jnp.bfloat16)
    return stacked.reshape(count_src * count_rcv, 2 * sources.shape[-1])


def local(spectra, src_ids):
    arrived = lax.all_to_all(spectra, "sta", split_axis=1, concat_axis=3, tiled=True)
    totals = block_sums(arrived)
    by_station = level_divide(arrived, jnp.pad(totals, ((0, 0), (0, 0), (1, 1))))
    hours_dev = by_station.shape[0]
    stations_dev = by_station.shape[1]
    transform = make_table(hours_dev * lax.axis_size("tm"))
    row_count = transform.shape[0] // lax.axis_size("tm")
    owners = src_ids[:, 0] // stations_dev
    offsets = src_ids - owners[:, None] * stations_dev
    results = []
    for step_no in range(ROUNDS):
        sources = spread(jnp.take(by_station, offsets[step_no], axis=1), "sta", owners[step_no])
        cross_spec = cross_block(sources, by_station)

        def project(first_row, row_span, cross_spec=cross_spec):
            return lax.dot_general(
                transform, cross_spec, (((1,), (1,)), ((), ())), preferred_element_type=jnp.float32
            )

        stacked = lax.psum_scatter(
            project(jnp.int32(0), row_count * lax.axis_size("tm")),
            "tm",
            scatter_dimension=0,
            tiled=True,
        )
        results.append(stacked.reshape(row_count, NSRC, stations_dev))
    return jnp.stack(results)


def solution(mesh):
    return jax.shard_map(
        local,
        mesh=mesh,
        in_specs=(P("tm", None, None, "sta"), P()),
        out_specs=P(None, "tm", None, "sta"),
        check_vma=False,
    )
```

profile of v0, /device:TPU:0, one launch (start us, length us, event | category | flops | bytes accessed | tf_op | source)
XLA Modules:
  0.0 453.4 jit_solution(4005050133008583266)
XLA Ops:
  6.5 7.0 %copy.32 = bf16[2,1024,2,512]{3,2,0,1:T(2,128)(2,1)} copy(bf16[2,1024,2,512]{3,2,1,0:T(2,128)(2,1)} %param.4) | data formatting | bytes 8388608 | tf_op args[0]
  21.9 19.0 %multiply_convert_fusion.1 = (bf16[256,4096]{1,0:T(8,128)(2,1)S(1)}, bf16[256,4096]{1,0:T(8,128)(2,1)}) fusion(s32[256]{0:T(256)S(1)} %iota_add_fusion), kind=kLoop, calls=%fused_computation.43 | loop fusion | flops 19922944 | bytes 4195328 | tf_op jit(solution)/shard_map/convert.15
  40.8 27.1 %all-to-all-done = bf16[2,1024,2,512]{3,2,0,1:T(2,128)(2,1)} async-done(((bf16[2,1024,2,512]{3,2,0,1:T(2,128)(2,1)}), bf16[2,1024,2,512]{3,2,0,1:T(2,128)(2,1)}, u32[]{:S(2)}, u32[]{:S(2)}) %all-to-all-start) | async-done | bytes 4194336 | tf_op jit(solution)/shard_map/all_to_all | solution.py:72
  75.4 8.7 %copy.34 = f32[2,128,2,8,512]{1,4,3,2,0:T(8,128)} copy(f32[2,128,2,8,512]{4,1,3,2,0:T(8,128)} %convert_bitcast_fusion) | data formatting | bytes 16777216 | tf_op jit(solution)/shard_map/convert_element_type | solution.py:36
  84.1 6.7 %fusion.13 = f32[2,128,1,4096]{1,3,2,0:T(8,128)} fusion(f32[2,128,2,4096]{1,3,2,0:T(8,128)} %bitcast.95), kind=kLoop, calls=%fused_computation.37 | loop fusion | flops 3145728 | bytes 12582912 | tf_op jit(solution)/shard_map/sqrt | solution.py:25
  90.8 13.3 %copy.36 = f32[2,128,2,4096]{3,2,1,0:T(2,128)} copy(f32[2,128,2,4096]{1,3,2,0:T(8,128)} %bitcast.96) | data formatting | bytes 16777216 | tf_op jit(solution)/shard_map/convert_element_type | solution.py:36
  109.1 5.7 %copy.35 = f32[2,128,4096]{2,1,0:T(8,128)} copy(f32[2,128,4096]{1,2,0:T(8,128)} %bitcast.108) | data formatting | bytes 8388608 | tf_op jit(solution)/shard_map/div | solution.py:37
  114.8 8.6 %divide_convert_fusion = bf16[2,128,2,4096]{3,2,1,0:T(2,128)(2,1)S(1)} fusion(f32[2,128,2,4096]{3,2,1,0:T(2,128)} %copy.36, f32[2,128,4096]{2,1,0:T(8,128)} %copy.35), kind=kLoop, calls=%fused_computation.28 | loop fusion | flops 4194304 | bytes 16777216 | tf_op jit(solution)/shard_map/convert_element_type | solution.py:38
  125.4 9.9 %fusion.28 = (f32[2,128,1,4096]{3,2,1,0:T(1,128)}, f32[2,128,1,4096]{3,2,1,0:T(1,128)}) fusion(bf16[2,128,2,4096]{3,2,1,0:T(2,128)(2,1)S(1)} %divide_convert_fusion), kind=kLoop, calls=%fused_computation.94 | loop fusion | bytes 16777216 | tf_op jit(solution)/shard_map/slice | solution.py:56
  148.1 14.8 %copy_bitcast_fusion = (f32[2,128,4096]{2,1,0:T(8,128)}, f32[2,128,4096]{2,1,0:T(8,128)}) fusion(f32[2,128,1,4096]{3,2,1,0:T(1,128)} %get-tuple-element.24, f32[2,128,1,4096]{3,2,1,0:T(1,128)} %get-tuple-element.23), kind=kLoop, calls=%fused_computation.40 | loop fusion | bytes 16777216
  163.0 40.7 %all-reduce.4.cloned.1.call-done = (bf16[2,8,2,4096]{3,2,0,1:T(2,128)(2,1)}, bf16[2,8,2,4096]{3,2,0,1:T(2,128)(2,1)}, bf16[2,8,2,4096]{3,2,0,1:T(2,128)(2,1)}) async-done(((bf16[2,8,2,4096]{3,2,0,1:T(2,128)(2,1)}, bf16[2,8,2,4096]{3,2,0,1:T(2,128)(2,1)}, bf16[2,8,2,4096]{3,2,0,1:T(2,128)(2,1)}), (bf16[2,8,2,4096]{3,2,0,1:T(2,128)(2,1)}, bf16[2,8,2,4096]{3,2,0,1:T(2,128)(2,1)}, ...) | async-done | bytes 786448 | tf_op jit(solution)/shard_map/psum | solution.py:20
  205.5 22.2 %add_reduce_fusion.2 = (bf16[8,128,4096]{2,1,0:T(8,128)(2,1)}, bf16[8,128,4096]{2,1,0:T(8,128)(2,1)}) fusion(f32[2,128,4096]{2,1,0:T(8,128)} %get-tuple-element.42, f32[2,8,4096]{2,1,0:T(8,128)S(1)} %bitcast.111, f32[2,128,4096]{2,1,0:T(8,128)} %get-tuple-element.43, f32[2,8,4096]{2,1,0:T(8,128)S(1)} %bitcast.113), kind=kLoop, calls=%fused_computation.8 | loop fusion | flops 58720256 | bytes 25690112 | tf_op jit(solution)/shard_map/reduce_sum | solution.py:55
  227.7 13.7 %pad_maximum_fusion = bf16[8,128,2,4096]{3,1,0,2:T(8,128)(2,1)} fusion(bf16[8,128,1,4096]{3,1,0,2:T(8,128)(2,1)} %bitcast.100, bf16[8,128,1,4096]{3,1,0,2:T(8,128)(2,1)} %bitcast.99), kind=kLoop, calls=%fused_computation.18 | loop fusion | flops 8388608 | bytes 33554432 | tf_op jit(solution)/shard_map/stack | solution.py:67
  241.4 22.3 %copy.39 = bf16[8,128,2,4096]{1,0,3,2:T(8,128)(2,1)} copy(bf16[8,128,2,4096]{3,1,0,2:T(8,128)(2,1)} %pad_maximum_fusion) | data formatting | bytes 33554432 | tf_op jit(solution)/shard_map/stack | solution.py:67
  263.7 11.9 %fusion.6 = f32[256,1024]{1,0:T(8,128)} fusion(bf16[1024,8,8,128]{3,2,1,0:T(8,128)(2,1)} %bitcast.107, bf16[256,4096]{1,0:T(8,128)(2,1)} %get-tuple-element.36, bf16[256,4096]{1,0:T(8,128)(2,1)S(1)} %get-tuple-element.35), kind=kOutput, calls=%fused_computation.15 | convolution fusion | flops 4303355904 | bytes 22020096 | tf_op jit(solution)/shard_map/dot_general | solution.py:87
  276.6 22.3 %add_reduce_fusion.1 = (bf16[8,128,4096]{2,1,0:T(8,128)(2,1)}, bf16[8,128,4096]{2,1,0:T(8,128)(2,1)}) fusion(f32[2,8,4096]{2,1,0:T(8,128)S(1)} %bitcast.112, f32[2,8,4096]{2,1,0:T(8,128)S(1)} %bitcast.114, f32[2,128,4096]{2,1,0:T(8,128)} %get-tuple-element.42, f32[2,128,4096]{2,1,0:T(8,128)} %get-tuple-element.43), kind=kLoop, calls=%fused_computation.6 | loop fusion | flops 58720256 | bytes 25690112 | tf_op jit(solution)/shard_map/reduce_sum | solution.py:55
  298.9 13.8 %pad_maximum_fusion.1 = bf16[8,128,2,4096]{3,1,0,2:T(8,128)(2,1)} fusion(bf16[8,128,1,4096]{3,1,0,2:T(8,128)(2,1)} %bitcast.102, bf16[8,128,1,4096]{3,1,0,2:T(8,128)(2,1)} %bitcast.101), kind=kLoop, calls=%fused_computation.19 | loop fusion | flops 8388608 | bytes 33554432 | tf_op jit(solution)/shard_map/stack | solution.py:67
  312.6 22.3 %copy.42 = bf16[8,128,2,4096]{1,0,3,2:T(8,128)(2,1)} copy(bf16[8,128,2,4096]{3,1,0,2:T(8,128)(2,1)} %pad_maximum_fusion.1) | data formatting | bytes 33554432 | tf_op jit(solution)/shard_map/stack | solution.py:67
  335.8 11.9 %fusion.3 = f32[256,1024]{1,0:T(8,128)} fusion(bf16[1024,8,8,128]{3,2,1,0:T(8,128)(2,1)} %bitcast.105, bf16[256,4096]{1,0:T(8,128)(2,1)} %get-tuple-element.36, bf16[256,4096]{1,0:T(8,128)(2,1)S(1)} %get-tuple-element.35), kind=kOutput, calls=%fused_computation.12 | convolution fusion | flops 4303355904 | bytes 22020096 | tf_op jit(solution)/shard_map/dot_general | solution.py:87
  347.8 22.3 %add_reduce_fusion = (bf16[8,128,4096]{2,1,0:T(8,128)(2,1)}, bf16[8,128,4096]{2,1,0:T(8,128)(2,1)}) fusion(f32[2,8,4096]{2,1,0:T(8,128)S(1)} %bitcast.109, f32[2,8,4096]{2,1,0:T(8,128)S(1)} %bitcast.110, f32[2,128,4096]{2,1,0:T(8,128)} %get-tuple-element.42, f32[2,128,4096]{2,1,0:T(8,128)} %get-tuple-element.43), kind=kLoop, calls=%fused_computation.4 | loop fusion | flops 58720256 | bytes 25690112 | tf_op jit(solution)/shard_map/reduce_sum | solution.py:55
  370.1 13.7 %pad_maximum_fusion.2 = bf16[8,128,2,4096]{3,1,0,2:T(8,128)(2,1)} fusion(bf16[8,128,1,4096]{3,1,0,2:T(8,128)(2,1)} %bitcast.98, bf16[8,128,1,4096]{3,1,0,2:T(8,128)(2,1)} %bitcast.97), kind=kLoop, calls=%fused_computation.20 | loop fusion | flops 8388608 | bytes 33554432 | tf_op jit(solution)/shard_map/stack | solution.py:67
  383.9 22.3 %copy.45 = bf16[8,128,2,4096]{1,0,3,2:T(8,128)(2,1)} copy(bf16[8,128,2,4096]{3,1,0,2:T(8,128)(2,1)} %pad_maximum_fusion.2) | data formatting | bytes 33554432 | tf_op jit(solution)/shard_map/stack | solution.py:67
  406.1 11.9 %fusion = f32[256,1024]{1,0:T(8,128)} fusion(bf16[1024,8,8,128]{3,2,1,0:T(8,128)(2,1)} %bitcast.106, bf16[256,4096]{1,0:T(8,128)(2,1)} %get-tuple-element.36, bf16[256,4096]{1,0:T(8,128)(2,1)S(1)} %get-tuple-element.35), kind=kOutput, calls=%fused_computation.9 | convolution fusion | flops 4303355904 | bytes 22020096 | tf_op jit(solution)/shard_map/dot_general | solution.py:87
  420.1 24.5 %reduce-scatter.8.cloned.1.call-done = f32[64,1024]{1,0:T(8,128)} async-done(((f32[256,1024]{1,0:T(8,128)}), f32[64,1024]{1,0:T(8,128)}) %reduce-scatter.8.cloned.1.call-update) | async-done | bytes 262160 | tf_op jit(solution)/shard_map/reduce_scatter | solution.py:91
  (51 shorter events, 41.3 us)
Async XLA Ops:
  6.5 12.6 %copy-start.3 = (s32[3,8]{1,0:T(4,128)S(1)}, s32[3,8]{1,0:T(4,128)}, u32[]{:S(2)}) copy-start(s32[3,8]{1,0:T(4,128)} %param.5) | copy-start | bytes 292
  13.6 54.4 %all-to-all-start = ((bf16[2,1024,2,512]{3,2,0,1:T(2,128)(2,1)}), bf16[2,1024,2,512]{3,2,0,1:T(2,128)(2,1)}, u32[]{:S(2)}, u32[]{:S(2)}) async-start(bf16[2,1024,2,512]{3,2,0,1:T(2,128)(2,1)} %copy.32), calls=%async_computation | async-start | bytes 8388608 | tf_op jit(solution)/shard_map/all_to_all | solution.py:72
  18.8 184.9 %all-reduce.4.cloned.1.call-start = ((), (), s32[]{:S(2)}) async-start(), calls=%async_computation.7 | async-start | bytes 1572864 | tf_op jit(solution)/shard_map/psum | solution.py:20
  123.4 2.0 copy-start
  147.5 270.5 %reduce-scatter.4.cloned.1.call-start = ((), (), s32[]{:S(2)}) async-start(), calls=%async_computation.4 | async-start | bytes 1310720 | tf_op jit(solution)/shard_map/reduce_scatter | solution.py:91
  263.7 12.0 %copy-start.2 = (bf16[2,8,2,4096]{3,2,0,1:T(2,128)(2,1)S(1)}, bf16[2,8,2,4096]{3,2,0,1:T(2,128)(2,1)}, u32[]{:S(2)}) copy-start(bf16[2,8,2,4096]{3,2,0,1:T(2,128)(2,1)} %get-tuple-element.15) | copy-start | bytes 786436
  275.7 143.4 %reduce-scatter.6.cloned.1.call-start = ((), (), s32[]{:S(2)}) async-start(), calls=%async_computation.5 | async-start | bytes 1310720 | tf_op jit(solution)/shard_map/reduce_scatter | solution.py:91
  312.6 22.3 %copy-start.1 = (bf16[2,8,2,4096]{3,2,0,1:T(2,128)(2,1)S(1)}, bf16[2,8,2,4096]{3,2,0,1:T(2,128)(2,1)}, u32[]{:S(2)}) copy-start(bf16[2,8,2,4096]{3,2,0,1:T(2,128)(2,1)} %get-tuple-element.16) | copy-start | bytes 786436
  347.7 96.9 %reduce-scatter.8.cloned.1.call-start = ((), (), s32[]{:S(2)}) async-start(), calls=%async_computation.6 | async-start | bytes 1310720 | tf_op jit(solution)/shard_map/reduce_scatter | solution.py:91
Sparse Core Ops, SparseCore 0:
  147.7 55.9 all-reduce.3
  275.8 26.4 reduce-scatter.3
  347.8 26.4 reduce-scatter.5
  418.2 26.4 reduce-scatter.7
where the time goes:
time: 459 us; the launch traced here: 453 us
  other arithmetic  153 us (33%)
  local copies, waits for them, and re-layouts  150 us (33%)
  waiting for transfers between devices  92.4 us (20%)
  matrix products  35.7 us (8%)
  between operations  15.5 us (3%)
  starting transfers between devices  6.15 us (1%)
    another operation x3, local copies, waits for them, and re-layouts, cross_block(): stacked = jnp.stack([real_part, imag_part], axis=2).astype(jnp.bfloat16)  66.9 us
    reduce_sum x3, other arithmetic, cross_block(): jnp.sum(source_f[:, :, None, 0] * receive_f[:, None, :, 0] + source_f[:,...  66.8 us
    another operation x3, other arithmetic, cross_block(): stacked = jnp.stack([real_part, imag_part], axis=2).astype(jnp.bfloat16)  41.2 us
    psum x1, waiting for transfers between devices, spread(): return lax.psum(jnp.where(mine, value, jnp.zeros_like(value)), axis)  40.7 us
    dot_general x3, matrix products, project(): lax.dot_general(transform, cross_spec, (((1,), (1,)), ((), ())), preferre...  35.7 us
    all_to_all x1, waiting for transfers between devices, local(): lax.all_to_all(spectra, 'sta', split_axis=1, concat_axis=3, tiled=True)  27.1 us
    unnamed x13, local copies, waits for them, and re-layouts  26.9 us
    reduce_scatter x3, waiting for transfers between devices, local(): lax.psum_scatter(project(jnp.int32(0), row_count * lax.axis_size('tm')),...  24.6 us
  transfers between devices with their start and end apart: 5, of which 3 were waited for; matrix products, arithmetic and copies ran while one was open for 39% of the time, Pallas kernels for 0%

commit v1 on v0

v1 whole, which is shorter than its diff:
```python
import functools
import math

import jax
import jax.numpy as jnp
from jax import lax
from jax.experimental import pallas as pl
from jax.experimental.pallas import tpu as pltpu
from jax.sharding import PartitionSpec as P

BINS = 4096
BLOCK = 64
LAGS = 256
NSRC = 8
ROUNDS = 3
HR_DEV = 2
EPSILON = 1e-05
SPLIT = 2
COLS = 128


def make_table(chunk_num, total_hours):
    bins_chunk = BINS // chunk_num
    shape = (chunk_num, bins_chunk, LAGS)
    freq = lax.broadcasted_iota(jnp.int32, shape, 0) * bins_chunk + lax.broadcasted_iota(jnp.int32, shape, 1)
    lag = lax.broadcasted_iota(jnp.int32, shape, 2) - LAGS // 2
    phase = jnp.bitwise_and(lag * freq, 2 * BINS - 1)
    angle = 2.0 * math.pi / (2 * BINS) * phase.astype(jnp.float32)
    scale = 1.0 / math.sqrt(BINS * total_hours)
    return jnp.concatenate([jnp.cos(angle) * scale, -jnp.sin(angle) * scale], axis=1).astype(jnp.bfloat16)


def split3(value):
    high = value.astype(jnp.bfloat16)
    rest = value - high.astype(jnp.float32)
    middle = rest.astype(jnp.bfloat16)
    low = (rest - middle.astype(jnp.float32)).astype(jnp.bfloat16)
    return high, middle, low


def exact_dot(value, ones):
    return sum(jnp.dot(part, ones, preferred_element_type=jnp.float32) for part in split3(value))


def inverse_levels(src_ref, inv_ref):
    chunk_num, hours, _, rows, width = src_ref.shape
    for hour in range(hours):

        def add_chunk(chunk, total, hour=hour):
            real = src_ref[chunk, hour, 0].astype(jnp.float32)
            imag = src_ref[chunk, hour, 1].astype(jnp.float32)
            magnitude = jnp.minimum(jnp.sqrt(real * real + imag * imag), 2.0**127)
            block = (lax.broadcasted_iota(jnp.int32, (width, COLS), 0) + chunk * width) // BLOCK
            away = block - lax.broadcasted_iota(jnp.int32, (width, COLS), 1)
            near = jnp.where((away >= -1) & (away <= 1), 1.0, 0.0).astype(jnp.bfloat16)
            return total + exact_dot(magnitude, near)

        total = lax.fori_loop(0, chunk_num, add_chunk, jnp.zeros((rows, COLS), jnp.float32))
        inv_ref[hour] = 1.0 / (total / (3.0 * BLOCK) + EPSILON)


def expand(inv_ref, chunk, width, hour):
    block = (lax.broadcasted_iota(jnp.int32, (COLS, width), 1) + chunk * width) // BLOCK
    same = jnp.where(block == lax.broadcasted_iota(jnp.int32, (COLS, width), 0), 1.0, 0.0)
    return exact_dot(inv_ref[hour], same.astype(jnp.bfloat16))


def correlate_kernel(x_ref, y_ref, t_ref, o_ref, inv_x, inv_y, xw, yw, yb, cross_a, cross_b, total):
    chunk = pl.program_id(0)
    chunk_num, hours, _, rows, width = x_ref.shape
    sources = y_ref.shape[3]

    @pl.when(chunk == 0)
    def _():
        inverse_levels(x_ref, inv_x)
        inverse_levels(y_ref, inv_y)
        total[...] = jnp.zeros_like(total)

    for hour in range(hours):
        scale_x = expand(inv_x, chunk, width, hour)
        scale_y = expand(inv_y, chunk, width, hour)
        for part in range(2):
            xw[hour, part] = (x_ref[chunk, hour, part].astype(jnp.float32) * scale_x).astype(jnp.bfloat16)
            yw[hour * 2 + part] = y_ref[chunk, hour, part].astype(jnp.float32) * scale_y

    def spread_source(k, carry):
        for piece in range(2 * hours):
            row = yw[piece, pl.ds(k, 1), :]
            yb[k, piece] = jnp.broadcast_to(row, (16, width)).astype(jnp.bfloat16)
        return carry

    lax.fori_loop(0, sources, spread_source, 0)

    for step in range(ROUNDS):
        cross = (cross_a, cross_b)[step % 2]
        for k in range(NSRC):
            for low in range(0, width, 128):
                lanes = slice(low, low + 128)
                y = [yb[step * NSRC + k, piece, :, lanes][None] for piece in range(2 * hours)]
                x = [xw[piece // 2, piece % 2, :, lanes].reshape(rows // 16, 16, 128) for piece in range(2 * hours)]
                real = (y[0] * x[0] + y[1] * x[1]) + (y[2] * x[2] + y[3] * x[3])
                imag = (y[1] * x[0] - y[0] * x[1]) + (y[3] * x[2] - y[2] * x[3])
                cross[k * rows:(k + 1) * rows, lanes] = real.reshape(rows, 128)
                cross[k * rows:(k + 1) * rows, width + low:width + low + 128] = imag.reshape(rows, 128)
        total[step] += jnp.dot(cross[...], t_ref[0], preferred_element_type=jnp.float32)

    @pl.when(chunk == chunk_num - 1)
    def _():
        for step in range(ROUNDS):
            o_ref[:, step * NSRC * rows:(step + 1) * NSRC * rows] = total[step].T.astype(jnp.bfloat16)


def correlate(x, y, table):
    chunk_num, hours, _, rows, width = x.shape
    sources = y.shape[3]
    whole = lambda shape: pl.BlockSpec(shape, lambda i: (0,) * len(shape))
    return pl.pallas_call(
        correlate_kernel,
        grid=(chunk_num,),
        in_specs=[
            whole(x.shape),
            whole(y.shape),
            pl.BlockSpec((1, 2 * width, LAGS), lambda i: (i, 0, 0)),
        ],
        out_specs=whole((LAGS, sources * rows)),
        out_shape=jax.ShapeDtypeStruct((LAGS, sources * rows), jnp.bfloat16),
        scratch_shapes=[
            pltpu.VMEM((hours, rows, COLS), jnp.float32),
            pltpu.VMEM((hours, sources, COLS), jnp.float32),
            pltpu.VMEM((hours, 2, rows, width), jnp.bfloat16),
            pltpu.VMEM((2 * hours, sources, width), jnp.float32),
            pltpu.VMEM((sources, 2 * hours, 16, width), jnp.bfloat16),
            pltpu.VMEM((NSRC * rows, 2 * width), jnp.bfloat16),
            pltpu.VMEM((NSRC * rows, 2 * width), jnp.bfloat16),
            pltpu.VMEM((ROUNDS, NSRC * rows, LAGS), jnp.float32),
        ],
        compiler_params=pltpu.CompilerParams(
            dimension_semantics=("arbitrary",), vmem_limit_bytes=48 * 1024 * 1024
        ),
        cost_estimate=pl.CostEstimate(
            flops=2 * LAGS * sources * rows * 2 * BINS * 2, bytes_accessed=12 * 1024 * 1024, transcendentals=0
        ),
    )(x, y, table)


def local(spectra, src_ids):
    hours, stations, _, width = spectra.shape
    chunk_num = BINS // width
    tm = lax.axis_size("tm")
    dev_rows = stations // chunk_num
    rows = dev_rows // SPLIT
    picked = jnp.take(spectra, src_ids.reshape(-1), axis=1).transpose(0, 2, 1, 3)
    y = lax.all_gather(picked, "sta", axis=0, tiled=False)
    parted = spectra.reshape(hours, chunk_num, SPLIT, rows, 2, width).transpose(2, 1, 0, 4, 3, 5)
    table = make_table(chunk_num, hours * tm)
    results = []
    for half in range(SPLIT):
        x = lax.all_to_all(parted[half], "sta", split_axis=0, concat_axis=0, tiled=True)
        partial = correlate(x, y, table)
        stacked = lax.psum_scatter(partial, "tm", scatter_dimension=0, tiled=True)
        results.append(stacked.reshape(LAGS // tm, ROUNDS, NSRC, rows))
    joined = jnp.concatenate(results, axis=3).astype(jnp.float32)
    return joined.transpose(1, 0, 2, 3)


def solution(mesh):
    return jax.shard_map(
        local,
        mesh=mesh,
        in_specs=(P("tm", None, None, "sta"), P()),
        out_specs=P(None, "tm", None, "sta"),
        check_vma=False,
    )
```

time: 459 us -> 202 us (0.44); the launches traced: 453 us -> 201 us
  local copies, waits for them, and re-layouts: 150 us -> 11.6 us
  other arithmetic: 153 us -> 23.9 us
  Pallas kernels: 0 us -> 80.3 us
  waiting for transfers between devices: 92.4 us -> 26.8 us
  matrix products: 35.7 us -> 0 us
  blocking collectives: 0 us -> 35.1 us
    pallas_call x0 -> x2, Pallas kernels: none -> 80.3 us  [correlate(): pl.pallas_call(correlate_kernel, grid=(chunk_num,), in_specs=[whole(x.sha...]
    reduce_sum x4 -> x0, other arithmetic: 69.6 us -> none  [the longest x3 66.8 us: cross_block(): jnp.sum(source_f[:, :, None, 0] * receive_f[:, None, :, 0] + source_f[:,...]
    another operation x3 -> x0, local copies, waits for them, and re-layouts: 66.9 us -> none  [cross_block(): stacked = jnp.stack([real_part, imag_part], axis=2).astype(jnp.bfloat16)]
    another operation x5 -> x1, other arithmetic: 61.2 us -> 18.2 us  [the longest x3 41.2 us: cross_block(): stacked = jnp.stack([real_part, imag_part], axis=2).astype(jnp.bfloat16)]
    psum x1 -> x0, waiting for transfers between devices: 40.7 us -> none  [spread(): return lax.psum(jnp.where(mine, value, jnp.zeros_like(value)), axis)]
    dot_general x3 -> x0, matrix products: 35.7 us -> none  [project(): lax.dot_general(transform, cross_spec, (((1,), (1,)), ((), ())), preferre...]
    all_gather x0 -> x1, blocking collectives: none -> 35.1 us  [local(): y = lax.all_gather(picked, 'sta', axis=0, tiled=False)]
    unnamed x13 -> x2, local copies, waits for them, and re-layouts: 26.9 us -> 0.01 us
  transfers between devices with their start and end apart: 5 -> 4, of which waited for: 3 -> 2; matrix products, arithmetic and copies ran while one was open for 39% -> 14% of each run, Pallas kernels for 0% -> 40%
where the time goes in v1:
time: 202 us; the launch traced here: 201 us
  Pallas kernels  80.3 us (40%)
  blocking collectives  35.1 us (17%)
  waiting for transfers between devices  26.8 us (13%)
  other arithmetic  23.9 us (12%)
  between operations  13.5 us (7%)
  local copies, waits for them, and re-layouts  11.6 us (6%)
  starting transfers between devices  9.9 us (5%)
    pallas_call x2, Pallas kernels, correlate(): pl.pallas_call(correlate_kernel, grid=(chunk_num,), in_specs=[whole(x.sha...  80.3 us
    all_gather x1, blocking collectives, local(): y = lax.all_gather(picked, 'sta', axis=0, tiled=False)  35.1 us
    reduce_scatter x2, waiting for transfers between devices, local(): stacked = lax.psum_scatter(partial, 'tm', scatter_dimension=0, tiled=True)  21.7 us
    another operation x1, other arithmetic  18.2 us
    all_to_all x2, starting transfers between devices, local(): lax.all_to_all(parted[half], 'sta', split_axis=0, concat_axis=0, tiled=True)  9.64 us
    all_to_all x2, waiting for transfers between devices, local(): lax.all_to_all(parted[half], 'sta', split_axis=0, concat_axis=0, tiled=True)  5.15 us
    concatenate x1, other arithmetic, make_table(): jnp.concatenate([jnp.cos(angle) * scale, -jnp.sin(angle) * scale], axis=1)  4.44 us
  transfers between devices with their start and end apart: 4, of which 2 were waited for; matrix products, arithmetic and copies ran while one was open for 14% of the time, Pallas kernels for 40%

profile of v1, /device:TPU:0, one launch (start us, length us, event | category | flops | bytes accessed | tf_op | source)
XLA Modules:
  0.0 201.2 jit_solution(5666826129353592152)
XLA Ops:
  6.5 3.2 %copy.16 = bf16[2,8,2,64,2,512]{5,3,4,0,1,2:T(8,128)(2,1)S(1)} copy(bf16[2,8,2,64,2,512]{5,4,3,2,1,0:T(2,128)(2,1)} %bitcast.18) | data formatting | bytes 8388608 | tf_op jit(solution)/shard_map/reshape | solution.py:154
  9.7 2.5 %slice_bitcast_fusion.1 = (bf16[8,2,2,64,512]{4,3,2,1,0:T(8,128)(2,1)}, bf16[8,2,2,64,512]{4,3,2,1,0:T(8,128)(2,1)}) fusion(bf16[2,8,2,2,64,512]{5,4,3,2,1,0:T(8,128)(2,1)S(1)} %bitcast.17), kind=kLoop, calls=%fused_computation.7 | loop fusion | bytes 8388608 | tf_op jit(solution)/shard_map/squeeze | solution.py:158
  12.2 5.3 %all-to-all-start = ((bf16[8,2,2,64,512]{4,3,2,1,0:T(8,128)(2,1)}), bf16[8,2,2,64,512]{4,3,2,1,0:T(8,128)(2,1)S(1)}, u32[]{:S(2)}, u32[]{:S(2)}) async-start(bf16[8,2,2,64,512]{4,3,2,1,0:T(8,128)(2,1)} %get-tuple-element.5), calls=%async_computation | async-start | bytes 4194304 | tf_op jit(solution)/shard_map/all_to_all | solution.py:158
  17.5 0.1 reshape.50
  17.6 0.1 reshape.49
  17.7 3.0 %gather_fusion = bf16[24,2,2,512]{3,2,1,0:T(2,128)(2,1)S(1)} fusion(bf16[2,1024,2,512]{3,2,1,0:T(2,128)(2,1)} %param.2, s32[1024]{0:T(1024)S(1)} %pad_clamp_fusion), kind=kCustom, calls=%fused_computation | custom fusion | bytes 196704 | tf_op jit(solution)/shard_map/jit(_take)/gather | solution.py:152
  20.7 0.2 fusion
  20.9 18.2 %multiply_convert_fusion.1 = (bf16[8,512,256]{2,1,0:T(8,128)(2,1)}, bf16[8,512,256]{2,1,0:T(8,128)(2,1)}) fusion(s32[8]{0:T(128)S(1)} %iota_multiply_fusion, s32[256]{0:T(256)S(1)} %iota_add_fusion), kind=kLoop, calls=%fused_computation.4 | loop fusion | flops 10485760 | bytes 4195360 | tf_op jit(solution)/shard_map/convert.1
  39.0 5.1 %all-to-all-done.x_ref = bf16[8,2,2,64,512]{4,3,2,1,0:T(8,128)(2,1)S(1)} async-done(((bf16[8,2,2,64,512]{4,3,2,1,0:T(8,128)(2,1)}), bf16[8,2,2,64,512]{4,3,2,1,0:T(8,128)(2,1)S(1)}, u32[]{:S(2)}, u32[]{:S(2)}) %all-to-all-start) | async-done | bytes 2097184 | tf_op jit(solution)/shard_map/all_to_all | solution.py:158
  44.2 4.3 %all-to-all-start.1 = ((bf16[8,2,2,64,512]{4,3,2,1,0:T(8,128)(2,1)}), bf16[8,2,2,64,512]{4,3,2,1,0:T(8,128)(2,1)}, u32[]{:S(2)}, u32[]{:S(2)}) async-start(bf16[8,2,2,64,512]{4,3,2,1,0:T(8,128)(2,1)} %get-tuple-element.6), calls=%async_computation.2 | async-start | bytes 4194304 | tf_op jit(solution)/shard_map/all_to_all | solution.py:158
  48.5 0.0 reduce-scatter.3.cloned.1.call-start
  48.6 35.1 %all-gather = bf16[16,2,24,512]{3,1,0,2:T(2,128)(2,1)S(1)} all-gather(bf16[2,2,24,512]{3,1,0,2:T(2,128)(2,1)S(1)} %fusion), channel_id=2, replica_groups=mesh['sta'=8,'tm'=4] {'sta'}, dimensions={0}, use_global_device_ids=true | all-gather | bytes 884736 | tf_op jit(solution)/shard_map/all_gather | solution.py:153
  83.7 0.4 copy.8
  84.1 4.4 %pad_maximum_fusion.t_ref = bf16[8,1024,256]{2,1,0:T(8,128)(2,1)} fusion(bf16[8,512,256]{2,1,0:T(8,128)(2,1)} %get-tuple-element.8, bf16[8,512,256]{2,1,0:T(8,128)(2,1)} %get-tuple-element.7), kind=kLoop, calls=%fused_computation.1 | loop fusion | flops 8388608 | bytes 8388608 | tf_op jit(solution)/shard_map/concatenate | solution.py:30
  88.6 39.8 %shard_map.28 = bf16[256,1536]{1,0:T(8,128)(2,1)} custom-call(bf16[8,2,2,64,512]{4,3,2,1,0:T(8,128)(2,1)S(1)} %all-to-all-done.x_ref, bf16[8,2,2,24,512]{4,3,2,1,0:T(8,128)(2,1)S(1)} %bitcast.15, bf16[8,1024,256]{2,1,0:T(8,128)(2,1)} %pad_maximum_fusion.t_ref), custom_call_target="tpu_custom_call" | custom-call | flops 12884901888 | bytes 12582912 | tf_op jit(solution)/shard_map/pallas_call | solution.py:117
  128.4 0.0 reduce-scatter.3.cloned.1.call-update
  128.4 0.2 reduce-scatter.5.cloned.1.call-start
  128.7 40.5 %shard_map.29 = bf16[256,1536]{1,0:T(8,128)(2,1)} custom-call(bf16[8,2,2,64,512]{4,3,2,1,0:T(8,128)(2,1)} %all-to-all-done.1.x_ref, bf16[8,2,2,24,512]{4,3,2,1,0:T(8,128)(2,1)S(1)} %bitcast.16, bf16[8,1024,256]{2,1,0:T(8,128)(2,1)} %pad_maximum_fusion.t_ref), custom_call_target="tpu_custom_call" | custom-call | flops 12884901888 | bytes 12582912 | tf_op jit(solution)/shard_map/pallas_call | solution.py:117
  169.2 0.0 reduce-scatter.5.cloned.1.call-update
  169.2 0.0 reduce-scatter.3.cloned.1.call-done
  169.2 1.2 reshape.51
  170.4 21.6 %reduce-scatter.5.cloned.1.call-done = bf16[64,1536]{1,0:T(8,128)(2,1)} async-done(((bf16[256,1536]{1,0:T(8,128)(2,1)}), bf16[64,1536]{1,0:T(8,128)(2,1)}) %reduce-scatter.5.cloned.1.call-update) | async-done | bytes 196624 | tf_op jit(solution)/shard_map/reduce_scatter | solution.py:160
  192.1 1.2 reshape.52
  193.2 1.1 convert_bitcast_fusion
  (8 shorter events, 0.0 us)
Async XLA Ops:
  12.2 5.3 %copy-start = (s32[3,8]{1,0:T(4,128)S(1)}, s32[3,8]{1,0:T(4,128)}, u32[]{:S(2)}) copy-start(s32[3,8]{1,0:T(4,128)} %param.3) | copy-start | bytes 292
  12.2 31.9 %all-to-all-start = ((bf16[8,2,2,64,512]{4,3,2,1,0:T(8,128)(2,1)}), bf16[8,2,2,64,512]{4,3,2,1,0:T(8,128)(2,1)S(1)}, u32[]{:S(2)}, u32[]{:S(2)}) async-start(bf16[8,2,2,64,512]{4,3,2,1,0:T(8,128)(2,1)} %get-tuple-element.5), calls=%async_computation | async-start | bytes 4194304 | tf_op jit(solution)/shard_map/all_to_all | solution.py:158
  44.2 84.5 %all-to-all-start.1 = ((bf16[8,2,2,64,512]{4,3,2,1,0:T(8,128)(2,1)}), bf16[8,2,2,64,512]{4,3,2,1,0:T(8,128)(2,1)}, u32[]{:S(2)}, u32[]{:S(2)}) async-start(bf16[8,2,2,64,512]{4,3,2,1,0:T(8,128)(2,1)} %get-tuple-element.6), calls=%async_computation.2 | async-start | bytes 4194304 | tf_op jit(solution)/shard_map/all_to_all | solution.py:158
  48.5 120.7 %reduce-scatter.3.cloned.1.call-start = ((), (), s32[]{:S(2)}) async-start(), calls=%async_computation.4 | async-start | bytes 983040 | tf_op jit(solution)/shard_map/reduce_scatter | solution.py:160
  128.4 63.6 %reduce-scatter.5.cloned.1.call-start = ((), (), s32[]{:S(2)}) async-start(), calls=%async_computation.5 | async-start | bytes 983040 | tf_op jit(solution)/shard_map/reduce_scatter | solution.py:160
Sparse Core Ops, SparseCore 0:
  128.5 22.7 reduce-scatter.2
  169.3 22.6 reduce-scatter.4

commit v2 on v1

v2 whole, which is shorter than its diff:
```python
import functools
import math

import jax
import jax.numpy as jnp
from jax import lax
from jax.experimental import pallas as pl
from jax.experimental.pallas import tpu as pltpu
from jax.sharding import PartitionSpec as P

BINS = 4096
BLOCK = 64
LAGS = 256
NSRC = 8
ROUNDS = 3
HR_DEV = 2
EPSILON = 1e-05
SPLIT = 2
COLS = 128


def make_table(chunk_num, total_hours):
    bins_chunk = BINS // chunk_num
    shape = (chunk_num, bins_chunk, LAGS)
    freq = lax.broadcasted_iota(jnp.int32, shape, 0) * bins_chunk + lax.broadcasted_iota(jnp.int32, shape, 1)
    lag = lax.broadcasted_iota(jnp.int32, shape, 2) - LAGS // 2
    phase = jnp.bitwise_and(lag * freq, 2 * BINS - 1)
    angle = 2.0 * math.pi / (2 * BINS) * phase.astype(jnp.float32)
    scale = 1.0 / math.sqrt(BINS * total_hours)
    return (jnp.cos(angle) * scale).astype(jnp.bfloat16), (-jnp.sin(angle) * scale).astype(jnp.bfloat16)


def split_wide(value):
    high = value.astype(jnp.bfloat16)
    low = (value - high.astype(jnp.float32)).astype(jnp.bfloat16)
    return jnp.concatenate([high, low], axis=-1)


def twice(ones):
    ones = ones.astype(jnp.bfloat16)
    return jnp.concatenate([ones, ones], axis=0)


def inverse_levels(src_ref, inv_ref):
    chunk_num, hours, _, rows, width = src_ref.shape

    def add_chunk(chunk, total):
        terms = []
        for hour in range(hours):
            real = src_ref[chunk, hour, 0].astype(jnp.float32)
            imag = src_ref[chunk, hour, 1].astype(jnp.float32)
            terms.append(split_wide(jnp.minimum(jnp.sqrt(real * real + imag * imag), 2.0**127)))
        block = (lax.broadcasted_iota(jnp.int32, (width, COLS), 0) + chunk * width) // BLOCK
        away = block - lax.broadcasted_iota(jnp.int32, (width, COLS), 1)
        near = twice(jnp.where((away >= -1) & (away <= 1), 1.0, 0.0))
        return total + jnp.dot(jnp.concatenate(terms, axis=0), near, preferred_element_type=jnp.float32)

    total = lax.fori_loop(0, chunk_num, add_chunk, jnp.zeros((hours * rows, COLS), jnp.float32))
    inv_ref[...] = split_wide(1.0 / (total / (3.0 * BLOCK) + EPSILON))


def expand(inv_ref, chunk, width):
    block = (lax.broadcasted_iota(jnp.int32, (COLS, width), 1) + chunk * width) // BLOCK
    same = twice(jnp.where(block == lax.broadcasted_iota(jnp.int32, (COLS, width), 0), 1.0, 0.0))
    return jnp.dot(inv_ref[...], same, preferred_element_type=jnp.float32)


def sources_kernel(y_ref, o_ref, inv_y):
    chunk_num, hours, _, rows, width = y_ref.shape
    inverse_levels(y_ref, inv_y)

    def one_chunk(chunk, carry):
        scale = expand(inv_y, chunk, width)
        for hour in range(hours):
            for part in range(2):
                piece = y_ref[chunk, hour, part].astype(jnp.float32) * scale[hour * rows:(hour + 1) * rows]
                o_ref[chunk, hour * 2 + part] = piece.astype(jnp.bfloat16).astype(jnp.float32)
        return carry

    lax.fori_loop(0, chunk_num, one_chunk, 0)


def whiten_sources(y):
    chunk_num, hours, parts, sources, width = y.shape
    return pl.pallas_call(
        sources_kernel,
        in_specs=[pl.BlockSpec(memory_space=pltpu.VMEM)],
        out_specs=pl.BlockSpec(memory_space=pltpu.VMEM),
        out_shape=jax.ShapeDtypeStruct((chunk_num, hours * parts, sources, width), jnp.float32),
        scratch_shapes=[pltpu.VMEM((hours * sources, 2 * COLS), jnp.bfloat16)],
        compiler_params=pltpu.CompilerParams(vmem_limit_bytes=24 * 1024 * 1024),
        cost_estimate=pl.CostEstimate(flops=400 * 1000 * 1000, bytes_accessed=3 * 1024 * 1024, transcendentals=0),
    )(y)


def correlate_kernel(x_ref, y_ref, tr_ref, ti_ref, o_ref, inv_x, xw, real_a, imag_a, real_b, imag_b, total):
    chunk = pl.program_id(0)
    chunk_num, hours, _, rows, width = x_ref.shape

    @pl.when(chunk == 0)
    def _():
        inverse_levels(x_ref, inv_x)
        total[...] = jnp.zeros_like(total)

    scale = expand(inv_x, chunk, width)
    for hour in range(hours):
        for part in range(2):
            piece = x_ref[chunk, hour, part].astype(jnp.float32) * scale[hour * rows:(hour + 1) * rows]
            xw[hour * 2 + part] = piece.astype(jnp.bfloat16)

    for step in range(ROUNDS):
        real_ref, imag_ref = ((real_a, imag_a), (real_b, imag_b))[step % 2]
        for k in range(NSRC):
            for low in range(0, width, 128):
                lanes = slice(low, low + 128)
                row = step * NSRC + k
                y = [
                    jnp.broadcast_to(y_ref[0, piece, row:row + 1, lanes], (16, 128)).astype(jnp.bfloat16)[None]
                    for piece in range(2 * hours)
                ]
                x = [xw[piece, :, lanes].reshape(rows // 16, 16, 128) for piece in range(2 * hours)]
                real = (y[0] * x[0] + y[1] * x[1]) + (y[2] * x[2] + y[3] * x[3])
                imag = (y[1] * x[0] - y[0] * x[1]) + (y[3] * x[2] - y[2] * x[3])
                real_ref[k * rows:(k + 1) * rows, lanes] = real.reshape(rows, 128)
                imag_ref[k * rows:(k + 1) * rows, lanes] = imag.reshape(rows, 128)
        total[step] += jnp.dot(real_ref[...], tr_ref[0], preferred_element_type=jnp.float32) + jnp.dot(
            imag_ref[...], ti_ref[0], preferred_element_type=jnp.float32
        )

    @pl.when(chunk == chunk_num - 1)
    def _():
        for step in range(ROUNDS):
            o_ref[:, step * NSRC * rows:(step + 1) * NSRC * rows] = total[step].T.astype(jnp.bfloat16)


def correlate(x, y, table):
    chunk_num, hours, _, rows, width = x.shape
    sources = y.shape[2]
    whole = lambda shape: pl.BlockSpec(shape, lambda i: (0,) * len(shape))
    cross = pltpu.VMEM((NSRC * rows, width), jnp.bfloat16)
    return pl.pallas_call(
        correlate_kernel,
        grid=(chunk_num,),
        in_specs=[
            whole(x.shape),
            pl.BlockSpec((1,) + y.shape[1:], lambda i: (i, 0, 0, 0)),
            pl.BlockSpec((1, width, LAGS), lambda i: (i, 0, 0)),
            pl.BlockSpec((1, width, LAGS), lambda i: (i, 0, 0)),
        ],
        out_specs=whole((LAGS, sources * rows)),
        out_shape=jax.ShapeDtypeStruct((LAGS, sources * rows), jnp.bfloat16),
        scratch_shapes=[
            pltpu.VMEM((hours * rows, 2 * COLS), jnp.bfloat16),
            pltpu.VMEM((hours * 2, rows, width), jnp.bfloat16),
            cross,
            cross,
            cross,
            cross,
            pltpu.VMEM((ROUNDS, NSRC * rows, LAGS), jnp.float32),
        ],
        compiler_params=pltpu.CompilerParams(
            dimension_semantics=("arbitrary",), vmem_limit_bytes=40 * 1024 * 1024
        ),
        cost_estimate=pl.CostEstimate(
            flops=2 * LAGS * sources * rows * 2 * BINS * 2, bytes_accessed=12 * 1024 * 1024, transcendentals=0
        ),
    )(x, y, *table)


def local(spectra, src_ids):
    hours, stations, _, width = spectra.shape
    chunk_num = BINS // width
    tm = lax.axis_size("tm")
    rows = stations // chunk_num // SPLIT
    picked = jnp.take(spectra, src_ids.reshape(-1), axis=1, mode="clip").transpose(0, 2, 1, 3)
    copies = jnp.broadcast_to(picked[None], (chunk_num,) + picked.shape)
    y = whiten_sources(lax.all_to_all(copies, "sta", split_axis=0, concat_axis=0, tiled=True))
    parted = spectra.reshape(hours, chunk_num, SPLIT, rows, 2, width)
    table = make_table(chunk_num, hours * tm)
    results = []
    for half in range(SPLIT):
        leaving = parted[:, :, half].transpose(1, 0, 3, 2, 4)
        x = lax.all_to_all(leaving, "sta", split_axis=0, concat_axis=0, tiled=True)
        partial = correlate(x, y, table)
        stacked = lax.psum_scatter(partial, "tm", scatter_dimension=0, tiled=True)
        results.append(stacked.reshape(LAGS // tm, ROUNDS, NSRC, rows))
    joined = jnp.concatenate(results, axis=3).astype(jnp.float32)
    return joined.transpose(1, 0, 2, 3)


def solution(mesh):
    return jax.shard_map(
        local,
        mesh=mesh,
        in_specs=(P("tm", None, None, "sta"), P()),
        out_specs=P(None, "tm", None, "sta"),
        check_vma=False,
    )
```

time: 202 us -> 167 us (0.83)
  blocking collectives: 35.1 us -> 0 us
  Pallas kernels: 80.3 us -> 48 us
  waiting for transfers between devices: 26.8 us -> 52.2 us
  local copies, waits for them, and re-layouts: 11.6 us -> 22.1 us
  other arithmetic: 23.9 us -> 17.7 us
  starting transfers between devices: 9.9 us -> 13.2 us
    pallas_call x2, Pallas kernels: 80.3 us -> 43.1 us  [correlate(): pl.pallas_call(correlate_kernel, grid=(chunk_num,), in_specs=[whole(x.sha...]
    all_gather x1 -> x0, blocking collectives: 35.1 us -> none  [local(): y = lax.all_gather(picked, 'sta', axis=0, tiled=False)]
    all_to_all x2 -> x3, waiting for transfers between devices: 5.15 us -> 28.3 us  [the longest x2 23.2 us: local(): x = lax.all_to_all(leaving, 'sta', split_axis=0, concat_axis=0, tiled=True)]
    another operation x1 -> x0, other arithmetic: 18.2 us -> none
    convert_element_type x0 -> x1, other arithmetic: none -> 16.6 us  [make_table(): (-jnp.sin(angle) * scale).astype(jnp.bfloat16)]
    unnamed x2 -> x14, local copies, waits for them, and re-layouts: 0.01 us -> 9.34 us
    slice x0 -> x1, local copies, waits for them, and re-layouts: none -> 5.67 us  [local(): leaving = parted[:, :, half].transpose(1, 0, 3, 2, 4)]
    pallas_call x0 -> x1, Pallas kernels: none -> 4.9 us  [whiten_sources(): pl.pallas_call(sources_kernel, in_specs=[pl.BlockSpec(memory_space=pltpu....]
  transfers between devices with their start and end apart: 4 -> 5, of which waited for: 2 -> 3; matrix products, arithmetic and copies ran while one was open for 14% -> 17% of each run, Pallas kernels for 40% -> 29%
where the time goes in v2:
time: 167 us
  waiting for transfers between devices  52.2 us (31%)
  Pallas kernels  48 us (29%)
  local copies, waits for them, and re-layouts  22.1 us (13%)
  other arithmetic  17.7 us (11%)
  between operations  13.5 us (8%)
  starting transfers between devices  13.2 us (8%)
    pallas_call x2, Pallas kernels, correlate(): pl.pallas_call(correlate_kernel, grid=(chunk_num,), in_specs=[whole(x.sha...  43.1 us
    reduce_scatter x2, waiting for transfers between devices, local(): stacked = lax.psum_scatter(partial, 'tm', scatter_dimension=0, tiled=True)  23.8 us
    all_to_all x2, waiting for transfers between devices, local(): x = lax.all_to_all(leaving, 'sta', split_axis=0, concat_axis=0, tiled=True)  23.2 us
    convert_element_type x1, other arithmetic, make_table(): (-jnp.sin(angle) * scale).astype(jnp.bfloat16)  16.6 us
    unnamed x14, local copies, waits for them, and re-layouts  9.34 us
    all_to_all x2, starting transfers between devices, local(): x = lax.all_to_all(leaving, 'sta', split_axis=0, concat_axis=0, tiled=True)  7.96 us
    slice x1, local copies, waits for them, and re-layouts, local(): leaving = parted[:, :, half].transpose(1, 0, 3, 2, 4)  5.67 us
    all_to_all x1, starting transfers between devices, local(): lax.all_to_all(copies, 'sta', split_axis=0, concat_axis=0, tiled=True)  5.17 us
  transfers between devices with their start and end apart: 5, of which 3 were waited for; matrix products, arithmetic and copies ran while one was open for 17% of the time, Pallas kernels for 29%

profile of v2, /device:TPU:0, one launch (start us, length us, event | category | flops | bytes accessed | tf_op | source)
XLA Modules:
  0.0 166.7 jit_solution(17086049884013495833)
XLA Ops:
  6.5 0.8 reshape.17
  7.3 3.0 %gather_fusion = bf16[24,2,2,512]{3,2,1,0:T(2,128)(2,1)S(1)} fusion(bf16[2,1024,2,512]{3,2,1,0:T(2,128)(2,1)} %param.2, s32[1024]{0:T(1024)S(1)} %pad_clamp_fusion), kind=kCustom, calls=%fused_computation | custom fusion | bytes 196704 | tf_op jit(solution)/shard_map/jit(_take)/gather | solution.py:175
  10.3 1.0 broadcast_in_dim.11
  11.3 5.2 %all-to-all-start.1 = ((bf16[8,2,2,24,512]{4,3,2,1,0:T(8,128)(2,1)}), bf16[8,2,2,24,512]{4,3,2,1,0:T(8,128)(2,1)S(1)}, u32[]{:S(2)}, u32[]{:S(2)}) async-start(bf16[8,2,2,24,512]{4,3,2,1,0:T(8,128)(2,1)} %broadcast_in_dim.11), calls=%async_computation.1 | async-start | bytes 1572864 | tf_op jit(solution)/shard_map/all_to_all | solution.py:177
  16.4 5.7 %fusion = (bf16[2,8,1,64,2,512]{5,4,3,2,1,0:T(2,128)(2,1)S(1)}, bf16[2,8,1,64,2,512]{5,4,3,2,1,0:T(2,128)(2,1)}) fusion(bf16[2,8,2,64,2,512]{5,4,3,2,1,0:T(2,128)(2,1)} %bitcast.16), kind=kLoop, calls=%fused_computation.11 | loop fusion | bytes 8388608 | tf_op jit(solution)/shard_map/slice | solution.py:182
  22.1 1.8 %copy.21 = bf16[2,8,1,64,2,512]{5,3,4,0,1,2:T(8,128)(2,1)} copy(bf16[2,8,1,64,2,512]{5,4,3,2,1,0:T(2,128)(2,1)S(1)} %get-tuple-element.5) | data formatting | bytes 4194304
  23.9 5.1 %all-to-all-done.1.y_ref = bf16[8,2,2,24,512]{4,3,2,1,0:T(8,128)(2,1)S(1)} async-done(((bf16[8,2,2,24,512]{4,3,2,1,0:T(8,128)(2,1)}), bf16[8,2,2,24,512]{4,3,2,1,0:T(8,128)(2,1)S(1)}, u32[]{:S(2)}, u32[]{:S(2)}) %all-to-all-start.1) | async-done | bytes 786464 | tf_op jit(solution)/shard_map/all_to_all | solution.py:177
  29.0 3.6 %all-to-all-start = ((bf16[8,2,2,64,512]{4,3,2,1,0:T(8,128)(2,1)}), bf16[8,2,2,64,512]{4,3,2,1,0:T(8,128)(2,1)S(1)}, u32[]{:S(2)}, u32[]{:S(2)}) async-start(bf16[8,2,2,64,512]{4,3,2,1,0:T(8,128)(2,1)} %bitcast.15), calls=%async_computation | async-start | bytes 4194304 | tf_op jit(solution)/shard_map/all_to_all | solution.py:183
  32.6 3.4 %copy.20 = bf16[2,8,1,64,2,512]{5,3,4,0,1,2:T(8,128)(2,1)} copy(bf16[2,8,1,64,2,512]{5,4,3,2,1,0:T(2,128)(2,1)} %get-tuple-element.6) | data formatting | bytes 4194304
  36.0 23.2 %all-to-all-done.x_ref = bf16[8,2,2,64,512]{4,3,2,1,0:T(8,128)(2,1)S(1)} async-done(((bf16[8,2,2,64,512]{4,3,2,1,0:T(8,128)(2,1)}), bf16[8,2,2,64,512]{4,3,2,1,0:T(8,128)(2,1)S(1)}, u32[]{:S(2)}, u32[]{:S(2)}) %all-to-all-start) | async-done | bytes 2097184 | tf_op jit(solution)/shard_map/all_to_all | solution.py:183
  59.2 4.4 %all-to-all-start.2 = ((bf16[8,2,2,64,512]{4,3,2,1,0:T(8,128)(2,1)}), bf16[8,2,2,64,512]{4,3,2,1,0:T(8,128)(2,1)}, u32[]{:S(2)}, u32[]{:S(2)}) async-start(bf16[8,2,2,64,512]{4,3,2,1,0:T(8,128)(2,1)} %bitcast.14), calls=%async_computation.3 | async-start | bytes 4194304 | tf_op jit(solution)/shard_map/all_to_all | solution.py:183
  63.6 0.0 reduce-scatter.3.cloned.1.call-start
  63.6 16.6 %multiply_convert_fusion = (bf16[8,512,256]{2,1,0:T(8,128)(2,1)S(1)}, bf16[8,512,256]{2,1,0:T(8,128)(2,1)S(1)}) fusion(s32[8]{0:T(128)S(1)} %iota_multiply_fusion, s32[256]{0:T(256)S(1)} %iota_add_fusion), kind=kLoop, calls=%fused_computation.1 | loop fusion | flops 10485760 | bytes 4195360 | tf_op jit(solution)/shard_map/convert_element_type | solution.py:30
  80.3 4.9 %shard_map.28.y_ref = f32[8,4,24,512]{3,2,1,0:T(8,128)S(1)} custom-call(bf16[8,2,2,24,512]{4,3,2,1,0:T(8,128)(2,1)S(1)} %all-to-all-done.1.y_ref), custom_call_target="tpu_custom_call" | custom-call | flops 400000000 | bytes 3145728 | tf_op jit(solution)/shard_map/pallas_call | solution.py:85
  85.2 20.8 %shard_map.29 = bf16[256,1536]{1,0:T(8,128)(2,1)} custom-call(bf16[8,2,2,64,512]{4,3,2,1,0:T(8,128)(2,1)S(1)} %copy-done.3, f32[8,4,24,512]{3,2,1,0:T(8,128)S(1)} %shard_map.28.y_ref, bf16[8,512,256]{2,1,0:T(8,128)(2,1)S(1)} %get-tuple-element.8.tr_ref, bf16[8,512,256]{2,1,0:T(8,128)(2,1)S(1)} %get-tuple-element.7.ti_ref), custom_call_target="tpu_custom_call" | custom-call | flops 12884901888 | bytes 12582912 | tf_op jit(solution)/shard_map/pallas_call | solution.py:141
  106.0 1.1 copy-done.4
  107.2 0.0 reduce-scatter.5.cloned.1.call-start
  107.3 1.6 copy-done.1
  108.8 1.4 copy-done.5
  110.2 22.3 %shard_map.30 = bf16[256,1536]{1,0:T(8,128)(2,1)} custom-call(bf16[8,2,2,64,512]{4,3,2,1,0:T(8,128)(2,1)} %all-to-all-done.2.x_ref, f32[8,4,24,512]{3,2,1,0:T(8,128)S(1)} %copy-done.5, bf16[8,512,256]{2,1,0:T(8,128)(2,1)S(1)} %copy-done.1, bf16[8,512,256]{2,1,0:T(8,128)(2,1)S(1)} %get-tuple-element.7.ti_ref), custom_call_target="tpu_custom_call" | custom-call | flops 12884901888 | bytes 12582912 | tf_op jit(solution)/shard_map/pallas_call | solution.py:141
  132.6 1.2 reshape.13
  133.8 23.8 %reduce-scatter.5.cloned.1.call-done = bf16[64,1536]{1,0:T(8,128)(2,1)} async-done(((bf16[256,1536]{1,0:T(8,128)(2,1)}), bf16[64,1536]{1,0:T(8,128)(2,1)}) %reduce-scatter.5.cloned.1.call-update) | async-done | bytes 196624 | tf_op jit(solution)/shard_map/reduce_scatter | solution.py:185
  157.6 1.2 reshape.14
  158.8 1.1 convert_bitcast_fusion
  (17 shorter events, 0.1 us)
Async XLA Ops:
  11.3 17.8 %all-to-all-start.1 = ((bf16[8,2,2,24,512]{4,3,2,1,0:T(8,128)(2,1)}), bf16[8,2,2,24,512]{4,3,2,1,0:T(8,128)(2,1)S(1)}, u32[]{:S(2)}, u32[]{:S(2)}) async-start(bf16[8,2,2,24,512]{4,3,2,1,0:T(8,128)(2,1)} %broadcast_in_dim.11), calls=%async_computation.1 | async-start | bytes 1572864 | tf_op jit(solution)/shard_map/all_to_all | solution.py:177
  29.0 30.2 %all-to-all-start = ((bf16[8,2,2,64,512]{4,3,2,1,0:T(8,128)(2,1)}), bf16[8,2,2,64,512]{4,3,2,1,0:T(8,128)(2,1)S(1)}, u32[]{:S(2)}, u32[]{:S(2)}) async-start(bf16[8,2,2,64,512]{4,3,2,1,0:T(8,128)(2,1)} %bitcast.15), calls=%async_computation | async-start | bytes 4194304 | tf_op jit(solution)/shard_map/all_to_all | solution.py:183
  59.2 4.4 %copy-start.2 = (bf16[8,2,2,64,512]{4,3,2,1,0:T(8,128)(2,1)}, bf16[8,2,2,64,512]{4,3,2,1,0:T(8,128)(2,1)S(1)}, u32[]{:S(2)}) copy-start(bf16[8,2,2,64,512]{4,3,2,1,0:T(8,128)(2,1)S(1)} %all-to-all-done.x_ref) | copy-start | bytes 6291460
  59.2 48.0 %all-to-all-start.2 = ((bf16[8,2,2,64,512]{4,3,2,1,0:T(8,128)(2,1)}), bf16[8,2,2,64,512]{4,3,2,1,0:T(8,128)(2,1)}, u32[]{:S(2)}, u32[]{:S(2)}) async-start(bf16[8,2,2,64,512]{4,3,2,1,0:T(8,128)(2,1)} %bitcast.14), calls=%async_computation.3 | async-start | bytes 4194304 | tf_op jit(solution)/shard_map/all_to_all | solution.py:183
  63.6 69.0 %reduce-scatter.3.cloned.1.call-start = ((), (), s32[]{:S(2)}) async-start(), calls=%async_computation.5 | async-start | bytes 983040 | tf_op jit(solution)/shard_map/reduce_scatter | solution.py:185
  63.6 21.6 %copy-start.3 = (bf16[8,2,2,64,512]{4,3,2,1,0:T(8,128)(2,1)S(1)}, bf16[8,2,2,64,512]{4,3,2,1,0:T(8,128)(2,1)}, u32[]{:S(2)}) copy-start(bf16[8,2,2,64,512]{4,3,2,1,0:T(8,128)(2,1)} %copy-done.2) | copy-start | bytes 6291460
  80.3 4.9 %copy-start = (bf16[8,512,256]{2,1,0:T(8,128)(2,1)}, bf16[8,512,256]{2,1,0:T(8,128)(2,1)S(1)}, u32[]{:S(2)}) copy-start(bf16[8,512,256]{2,1,0:T(8,128)(2,1)S(1)} %get-tuple-element.8.tr_ref) | copy-start | bytes 6291460
  106.0 1.2 copy-start.4
  107.2 50.4 %reduce-scatter.5.cloned.1.call-start = ((), (), s32[]{:S(2)}) async-start(), calls=%async_computation.6 | async-start | bytes 983040 | tf_op jit(solution)/shard_map/reduce_scatter | solution.py:185
  107.2 1.6 copy-start.1
  108.8 1.4 copy-start.5
Sparse Core Ops, SparseCore 0:
  107.3 24.9 reduce-scatter.2
  134.6 22.9 reduce-scatter.4

commit v3 on v2

--- a/solution.py
+++ b/solution.py
@@ -15,7 +15,7 @@
 ROUNDS = 3
 HR_DEV = 2
 EPSILON = 1e-05
-SPLIT = 2
+PARTS = (3, 3, 2)
 COLS = 128
 
 
@@ -88,7 +88,7 @@
         out_specs=pl.BlockSpec(memory_space=pltpu.VMEM),
         out_shape=jax.ShapeDtypeStruct((chunk_num, hours * parts, sources, width), jnp.float32),
         scratch_shapes=[pltpu.VMEM((hours * sources, 2 * COLS), jnp.bfloat16)],
-        compiler_params=pltpu.CompilerParams(vmem_limit_bytes=24 * 1024 * 1024),
+        compiler_params=pltpu.CompilerParams(vmem_limit_bytes=16 * 1024 * 1024),
         cost_estimate=pl.CostEstimate(flops=400 * 1000 * 1000, bytes_accessed=3 * 1024 * 1024, transcendentals=0),
     )(y)
 
@@ -159,7 +159,7 @@
             pltpu.VMEM((ROUNDS, NSRC * rows, LAGS), jnp.float32),
         ],
         compiler_params=pltpu.CompilerParams(
-            dimension_semantics=("arbitrary",), vmem_limit_bytes=40 * 1024 * 1024
+            dimension_semantics=("arbitrary",), vmem_limit_bytes=24 * 1024 * 1024
         ),
         cost_estimate=pl.CostEstimate(
             flops=2 * LAGS * sources * rows * 2 * BINS * 2, bytes_accessed=12 * 1024 * 1024, transcendentals=0
@@ -171,16 +171,23 @@
     hours, stations, _, width = spectra.shape
     chunk_num = BINS // width
     tm = lax.axis_size("tm")
-    rows = stations // chunk_num // SPLIT
+    dev_rows = stations // chunk_num
     picked = jnp.take(spectra, src_ids.reshape(-1), axis=1, mode="clip").transpose(0, 2, 1, 3)
     copies = jnp.broadcast_to(picked[None], (chunk_num,) + picked.shape)
     y = whiten_sources(lax.all_to_all(copies, "sta", split_axis=0, concat_axis=0, tiled=True))
-    parted = spectra.reshape(hours, chunk_num, SPLIT, rows, 2, width)
+    parted = spectra.reshape(hours, chunk_num, dev_rows, 2, width)
     table = make_table(chunk_num, hours * tm)
-    results = []
-    for half in range(SPLIT):
-        leaving = parted[:, :, half].transpose(1, 0, 3, 2, 4)
-        x = lax.all_to_all(leaving, "sta", split_axis=0, concat_axis=0, tiled=True)
+    arrived, results = [], []
+    first = 0
+    for number, share in enumerate(PARTS):
+        rows = dev_rows * share // sum(PARTS)
+        leaving = parted[:, :, first:first + rows].transpose(1, 0, 3, 2, 4)
+        first += rows
+        if number == 1:
+            leaving, y, table = lax.optimization_barrier((leaving, y, table))
+        arrived.append(lax.all_to_all(leaving, "sta", split_axis=0, concat_axis=0, tiled=True))
+    for x in arrived:
+        rows = x.shape[3]
         partial = correlate(x, y, table)
         stacked = lax.psum_scatter(partial, "tm", scatter_dimension=0, tiled=True)
         results.append(stacked.reshape(LAGS // tm, ROUNDS, NSRC, rows))

time: 167 us -> 179 us (1.072)
  waiting for transfers between devices: 52.2 us -> 40.1 us
  local copies, waits for them, and re-layouts: 22.1 us -> 33.7 us
  Pallas kernels: 48 us -> 55.7 us
  starting transfers between devices: 13.2 us -> 17.6 us
    all_to_all x2 -> x3, waiting for transfers between devices: 23.2 us -> 8.66 us  [local(): lax.all_to_all(leaving, 'sta', split_axis=0, concat_axis=0, tiled=True)]
    pallas_call x2 -> x3, Pallas kernels: 43.1 us -> 50.8 us  [correlate(): pl.pallas_call(correlate_kernel, grid=(chunk_num,), in_specs=[whole(x.sha...]
    unnamed x14 -> x21, local copies, waits for them, and re-layouts: 9.34 us -> 17 us
    all_to_all x1, waiting for transfers between devices: 5.13 us -> 9.4 us  [local(): lax.all_to_all(copies, 'sta', split_axis=0, concat_axis=0, tiled=True)]
    all_to_all x2 -> x3, starting transfers between devices: 7.96 us -> 12.2 us  [local(): lax.all_to_all(leaving, 'sta', split_axis=0, concat_axis=0, tiled=True)]
    reduce_scatter x2 -> x3, waiting for transfers between devices: 23.8 us -> 22 us  [local(): stacked = lax.psum_scatter(partial, 'tm', scatter_dimension=0, tiled=True)]
    slice x1 -> x2, local copies, waits for them, and re-layouts: 5.67 us -> 7.15 us  [local(): leaving = parted[:, :, first:first + rows].transpose(1, 0, 3, 2, 4)]
  transfers between devices with their start and end apart: 5 -> 7, of which waited for: 3 -> 4; matrix products, arithmetic and copies ran while one was open for 17% -> 18% of each run, Pallas kernels for 29% -> 31%
where the time goes in v3:
time: 179 us; the launch traced here: 178 us
  Pallas kernels  55.7 us (31%)
  waiting for transfers between devices  40.1 us (22%)
  local copies, waits for them, and re-layouts  33.7 us (19%)
  other arithmetic  17.7 us (10%)
  starting transfers between devices  17.6 us (10%)
  between operations  13.3 us (7%)
    pallas_call x3, Pallas kernels, correlate(): pl.pallas_call(correlate_kernel, grid=(chunk_num,), in_specs=[whole(x.sha...  50.8 us
    reduce_scatter x3, waiting for transfers between devices, local(): stacked = lax.psum_scatter(partial, 'tm', scatter_dimension=0, tiled=True)  22 us
    convert_element_type x1, other arithmetic, make_table(): (-jnp.sin(angle) * scale).astype(jnp.bfloat16)  17.3 us
    unnamed x21, local copies, waits for them, and re-layouts  17 us
    all_to_all x3, starting transfers between devices, local(): lax.all_to_all(leaving, 'sta', split_axis=0, concat_axis=0, tiled=True)  12.2 us
    all_to_all x1, waiting for transfers between devices, local(): lax.all_to_all(copies, 'sta', split_axis=0, concat_axis=0, tiled=True)  9.4 us
    all_to_all x3, waiting for transfers between devices, local(): lax.all_to_all(leaving, 'sta', split_axis=0, concat_axis=0, tiled=True)  8.66 us
    slice x2, local copies, waits for them, and re-layouts, local(): leaving = parted[:, :, first:first + rows].transpose(1, 0, 3, 2, 4)  7.15 us
  transfers between devices with their start and end apart: 7, of which 4 were waited for; matrix products, arithmetic and copies ran while one was open for 18% of the time, Pallas kernels for 31%

profile of v3, /device:TPU:0, one launch (start us, length us, event | category | flops | bytes accessed | tf_op | source)
XLA Modules:
  0.0 178.0 jit_solution(16055751604210365663)
XLA Ops:
  7.3 2.9 %gather_fusion = bf16[24,2,2,512]{3,2,1,0:T(2,128)(2,1)S(1)} fusion(bf16[2,1024,2,512]{3,2,1,0:T(2,128)(2,1)} %param.2, s32[1024]{0:T(1024)S(1)} %pad_clamp_fusion), kind=kCustom, calls=%fused_computation | custom fusion | bytes 196704 | tf_op jit(solution)/shard_map/jit(_take)/gather | solution.py:175
  11.3 5.2 %all-to-all-start.1 = ((bf16[8,2,2,24,512]{4,3,2,1,0:T(8,128)(2,1)}), bf16[8,2,2,24,512]{4,3,2,1,0:T(8,128)(2,1)S(1)}, u32[]{:S(2)}, u32[]{:S(2)}) async-start(bf16[8,2,2,24,512]{4,3,2,1,0:T(8,128)(2,1)} %broadcast_in_dim.11), calls=%async_computation.1 | async-start | bytes 1572864 | tf_op jit(solution)/shard_map/all_to_all | solution.py:177
  16.4 2.0 %slice.16 = bf16[2,8,32,2,512]{4,3,2,1,0:T(2,128)(2,1)S(1)} slice(bf16[2,8,128,2,512]{4,3,2,1,0:T(2,128)(2,1)} %bitcast.16), slice={[0:2], [0:8], [96:128], [0:2], [0:512]} | slice | bytes 2097152 | tf_op jit(solution)/shard_map/slice | solution.py:184
  19.6 9.4 %all-to-all-done.1.y_ref = bf16[8,2,2,24,512]{4,3,2,1,0:T(8,128)(2,1)S(1)} async-done(((bf16[8,2,2,24,512]{4,3,2,1,0:T(8,128)(2,1)}), bf16[8,2,2,24,512]{4,3,2,1,0:T(8,128)(2,1)S(1)}, u32[]{:S(2)}, u32[]{:S(2)}) %all-to-all-start.1) | async-done | bytes 786464 | tf_op jit(solution)/shard_map/all_to_all | solution.py:177
  29.0 3.6 %all-to-all-start.3 = ((bf16[8,2,2,32,512]{4,3,2,1,0:T(8,128)(2,1)}), bf16[8,2,2,32,512]{4,3,2,1,0:T(8,128)(2,1)S(1)}, u32[]{:S(2)}, u32[]{:S(2)}) async-start(bf16[8,2,2,32,512]{4,3,2,1,0:T(8,128)(2,1)} %bitcast.13), calls=%async_computation.5 | async-start | bytes 2097152 | tf_op jit(solution)/shard_map/all_to_all | solution.py:188
  32.6 5.2 %fusion = (bf16[2,8,48,2,512]{4,3,2,1,0:T(2,128)(2,1)S(1)}, bf16[2,8,48,2,512]{4,3,2,1,0:T(2,128)(2,1)}) fusion(bf16[2,8,128,2,512]{4,3,2,1,0:T(2,128)(2,1)} %bitcast.17), kind=kLoop, calls=%fused_computation.11 | loop fusion | bytes 6291456 | tf_op jit(solution)/shard_map/slice | solution.py:184
  37.7 1.5 copy.24
  39.3 8.7 %all-to-all-done.3.x_ref = bf16[8,2,2,32,512]{4,3,2,1,0:T(8,128)(2,1)S(1)} async-done(((bf16[8,2,2,32,512]{4,3,2,1,0:T(8,128)(2,1)}), bf16[8,2,2,32,512]{4,3,2,1,0:T(8,128)(2,1)S(1)}, u32[]{:S(2)}, u32[]{:S(2)}) %all-to-all-start.3) | async-done | bytes 1048608 | tf_op jit(solution)/shard_map/all_to_all | solution.py:188
  47.9 4.3 %all-to-all-start = ((bf16[8,2,2,48,512]{4,3,2,1,0:T(8,128)(2,1)}), bf16[8,2,2,48,512]{4,3,2,1,0:T(8,128)(2,1)}, u32[]{:S(2)}, u32[]{:S(2)}) async-start(bf16[8,2,2,48,512]{4,3,2,1,0:T(8,128)(2,1)} %bitcast.15), calls=%async_computation | async-start | bytes 3145728 | tf_op jit(solution)/shard_map/all_to_all | solution.py:188
  52.2 2.9 %copy.23 = bf16[2,8,48,2,512]{4,2,3,0,1:T(8,128)(2,1)} copy(bf16[2,8,48,2,512]{4,3,2,1,0:T(2,128)(2,1)} %get-tuple-element.14) | data formatting | bytes 3145728
  55.1 17.3 %multiply_convert_fusion = (bf16[8,512,256]{2,1,0:T(8,128)(2,1)S(1)}, bf16[8,512,256]{2,1,0:T(8,128)(2,1)}) fusion(s32[8]{0:T(128)S(1)} %iota_multiply_fusion, s32[256]{0:T(256)S(1)} %iota_add_fusion), kind=kLoop, calls=%fused_computation.1 | loop fusion | flops 10485760 | bytes 4195360 | tf_op jit(solution)/shard_map/convert_element_type | solution.py:30
  72.5 4.9 %shard_map.28.y_ref = f32[8,4,24,512]{3,2,1,0:T(8,128)S(1)} custom-call(bf16[8,2,2,24,512]{4,3,2,1,0:T(8,128)(2,1)S(1)} %all-to-all-done.1.y_ref), custom_call_target="tpu_custom_call" | custom-call | flops 400000000 | bytes 3145728 | tf_op jit(solution)/shard_map/pallas_call | solution.py:85
  78.6 4.3 %all-to-all-start.2 = ((bf16[8,2,2,48,512]{4,3,2,1,0:T(8,128)(2,1)}), bf16[8,2,2,48,512]{4,3,2,1,0:T(8,128)(2,1)}, u32[]{:S(2)}, u32[]{:S(2)}) async-start(bf16[8,2,2,48,512]{4,3,2,1,0:T(8,128)(2,1)} %bitcast.14), calls=%async_computation.3 | async-start | bytes 3145728 | tf_op jit(solution)/shard_map/all_to_all | solution.py:188
  82.9 1.6 copy-done
  84.5 1.4 copy-done.4
  87.2 13.5 %shard_map.31 = bf16[256,768]{1,0:T(8,128)(2,1)} custom-call(bf16[8,2,2,32,512]{4,3,2,1,0:T(8,128)(2,1)S(1)} %copy-done.8, f32[8,4,24,512]{3,2,1,0:T(8,128)S(1)} %copy-done.4, bf16[8,512,256]{2,1,0:T(8,128)(2,1)S(1)} %copy-done, bf16[8,512,256]{2,1,0:T(8,128)(2,1)S(1)} %get-tuple-element.11.ti_ref), custom_call_target="tpu_custom_call" | custom-call | flops 6442450944 | bytes 12582912 | tf_op jit(solution)/shard_map/pallas_call | solution.py:141
  100.8 1.6 copy-done.1
  102.4 1.4 copy-done.5
  103.8 18.6 %shard_map.29 = bf16[256,1152]{1,0:T(8,128)(2,1)} custom-call(bf16[8,2,2,48,512]{4,3,2,1,0:T(8,128)(2,1)} %all-to-all-done.x_ref, f32[8,4,24,512]{3,2,1,0:T(8,128)S(1)} %copy-done.5, bf16[8,512,256]{2,1,0:T(8,128)(2,1)S(1)} %copy-done.1, bf16[8,512,256]{2,1,0:T(8,128)(2,1)S(1)} %get-tuple-element.11.ti_ref), custom_call_target="tpu_custom_call" | custom-call | flops 9663676416 | bytes 12582912 | tf_op jit(solution)/shard_map/pallas_call | solution.py:141
  122.7 1.6 copy-done.2
  124.3 1.4 copy-done.6
  125.7 18.6 %shard_map.30 = bf16[256,1152]{1,0:T(8,128)(2,1)} custom-call(bf16[8,2,2,48,512]{4,3,2,1,0:T(8,128)(2,1)} %all-to-all-done.2.x_ref, f32[8,4,24,512]{3,2,1,0:T(8,128)S(1)} %copy-done.6, bf16[8,512,256]{2,1,0:T(8,128)(2,1)S(1)} %copy-done.2, bf16[8,512,256]{2,1,0:T(8,128)(2,1)S(1)} %get-tuple-element.11.ti_ref), custom_call_target="tpu_custom_call" | custom-call | flops 9663676416 | bytes 12582912 | tf_op jit(solution)/shard_map/pallas_call | solution.py:141
  146.3 1.3 reshape.16
  147.6 21.3 %reduce-scatter.6.cloned.1.call-done = bf16[64,1152]{1,0:T(8,128)(2,1)} async-done(((bf16[256,1152]{1,0:T(8,128)(2,1)}), bf16[64,1152]{1,0:T(8,128)(2,1)}) %reduce-scatter.6.cloned.1.call-update) | async-done | bytes 147472 | tf_op jit(solution)/shard_map/reduce_scatter | solution.py:192
  (34 shorter events, 10.2 us)
Async XLA Ops:
  11.3 17.8 %all-to-all-start.1 = ((bf16[8,2,2,24,512]{4,3,2,1,0:T(8,128)(2,1)}), bf16[8,2,2,24,512]{4,3,2,1,0:T(8,128)(2,1)S(1)}, u32[]{:S(2)}, u32[]{:S(2)}) async-start(bf16[8,2,2,24,512]{4,3,2,1,0:T(8,128)(2,1)} %broadcast_in_dim.11), calls=%async_computation.1 | async-start | bytes 1572864 | tf_op jit(solution)/shard_map/all_to_all | solution.py:177
  29.0 18.9 %all-to-all-start.3 = ((bf16[8,2,2,32,512]{4,3,2,1,0:T(8,128)(2,1)}), bf16[8,2,2,32,512]{4,3,2,1,0:T(8,128)(2,1)S(1)}, u32[]{:S(2)}, u32[]{:S(2)}) async-start(bf16[8,2,2,32,512]{4,3,2,1,0:T(8,128)(2,1)} %bitcast.13), calls=%async_computation.5 | async-start | bytes 2097152 | tf_op jit(solution)/shard_map/all_to_all | solution.py:188
  47.9 7.2 %copy-start.7 = (bf16[8,2,2,32,512]{4,3,2,1,0:T(8,128)(2,1)}, bf16[8,2,2,32,512]{4,3,2,1,0:T(8,128)(2,1)S(1)}, u32[]{:S(2)}) copy-start(bf16[8,2,2,32,512]{4,3,2,1,0:T(8,128)(2,1)S(1)} %all-to-all-done.3.x_ref) | copy-start | bytes 3145732
  47.9 30.6 %all-to-all-start = ((bf16[8,2,2,48,512]{4,3,2,1,0:T(8,128)(2,1)}), bf16[8,2,2,48,512]{4,3,2,1,0:T(8,128)(2,1)}, u32[]{:S(2)}, u32[]{:S(2)}) async-start(bf16[8,2,2,48,512]{4,3,2,1,0:T(8,128)(2,1)} %bitcast.15), calls=%async_computation | async-start | bytes 3145728 | tf_op jit(solution)/shard_map/all_to_all | solution.py:188
  77.4 1.2 copy-start.3
  78.6 44.1 %all-to-all-start.2 = ((bf16[8,2,2,48,512]{4,3,2,1,0:T(8,128)(2,1)}), bf16[8,2,2,48,512]{4,3,2,1,0:T(8,128)(2,1)}, u32[]{:S(2)}, u32[]{:S(2)}) async-start(bf16[8,2,2,48,512]{4,3,2,1,0:T(8,128)(2,1)} %bitcast.14), calls=%async_computation.3 | async-start | bytes 3145728 | tf_op jit(solution)/shard_map/all_to_all | solution.py:188
  82.9 61.4 %reduce-scatter.8.cloned.1.call-start = ((), (), s32[]{:S(2)}) async-start(), calls=%async_computation.9 | async-start | bytes 491520 | tf_op jit(solution)/shard_map/reduce_scatter | solution.py:192
  82.9 1.6 copy-start
  84.5 1.4 copy-start.4
  85.9 1.2 copy-start.8
  100.7 45.5 %reduce-scatter.4.cloned.1.call-start = ((), (), s32[]{:S(2)}) async-start(), calls=%async_computation.7 | async-start | bytes 737280 | tf_op jit(solution)/shard_map/reduce_scatter | solution.py:192
  100.8 1.6 copy-start.1
  102.4 1.4 copy-start.5
  122.5 46.4 %reduce-scatter.6.cloned.1.call-start = ((), (), s32[]{:S(2)}) async-start(), calls=%async_computation.8 | async-start | bytes 737280 | tf_op jit(solution)/shard_map/reduce_scatter | solution.py:192
  122.7 1.6 copy-start.2
  124.3 1.4 copy-start.6
Sparse Core Ops, SparseCore 0:
  100.9 22.1 reduce-scatter.7
  125.5 20.7 reduce-scatter.3
  148.7 20.2 reduce-scatter.5

commit v4 on v3

--- a/solution.py
+++ b/solution.py
@@ -15,7 +15,7 @@
 ROUNDS = 3
 HR_DEV = 2
 EPSILON = 1e-05
-PARTS = (3, 3, 2)
+PARTS = (1, 1)
 COLS = 128
 
 
@@ -159,7 +159,7 @@
             pltpu.VMEM((ROUNDS, NSRC * rows, LAGS), jnp.float32),
         ],
         compiler_params=pltpu.CompilerParams(
-            dimension_semantics=("arbitrary",), vmem_limit_bytes=24 * 1024 * 1024
+            dimension_semantics=("arbitrary",), vmem_limit_bytes=56 * 1024 * 1024
         ),
         cost_estimate=pl.CostEstimate(
             flops=2 * LAGS * sources * rows * 2 * BINS * 2, bytes_accessed=12 * 1024 * 1024, transcendentals=0
@@ -184,7 +184,7 @@
         leaving = parted[:, :, first:first + rows].transpose(1, 0, 3, 2, 4)
         first += rows
         if number == 1:
-            leaving, y, table = lax.optimization_barrier((leaving, y, table))
+            leaving, arrived[0], y, table = lax.optimization_barrier((leaving, arrived[0], y, table))
         arrived.append(lax.all_to_all(leaving, "sta", split_axis=0, concat_axis=0, tiled=True))
     for x in arrived:
         rows = x.shape[3]

time: 179 us -> 147 us (0.82)
  local copies, waits for them, and re-layouts: 33.7 us -> 17.9 us
  waiting for transfers between devices: 40.1 us -> 32 us
  Pallas kernels: 55.7 us -> 50.5 us
  starting transfers between devices: 17.6 us -> 13.2 us
    unnamed x21 -> x6, local copies, waits for them, and re-layouts: 17 us -> 6.08 us
    pallas_call x3 -> x2, Pallas kernels: 50.8 us -> 45.6 us  [correlate(): pl.pallas_call(correlate_kernel, grid=(chunk_num,), in_specs=[whole(x.sha...]
    all_to_all x3 -> x2, waiting for transfers between devices: 8.66 us -> 4.27 us  [local(): lax.all_to_all(leaving, 'sta', split_axis=0, concat_axis=0, tiled=True)]
    all_to_all x3 -> x2, starting transfers between devices: 12.2 us -> 7.96 us  [local(): lax.all_to_all(leaving, 'sta', split_axis=0, concat_axis=0, tiled=True)]
    all_to_all x1, waiting for transfers between devices: 9.4 us -> 6.06 us  [local(): lax.all_to_all(copies, 'sta', split_axis=0, concat_axis=0, tiled=True)]
    slice x2 -> x1, local copies, waits for them, and re-layouts: 7.15 us -> 4.72 us  [local(): leaving = parted[:, :, first:first + rows].transpose(1, 0, 3, 2, 4)]
    reduce_scatter x3 -> x2, waiting for transfers between devices: 22 us -> 21.7 us  [local(): stacked = lax.psum_scatter(partial, 'tm', scatter_dimension=0, tiled=True)]
  transfers between devices with their start and end apart: 7 -> 5, of which waited for: 4 -> 4; matrix products, arithmetic and copies ran while one was open for 18% -> 19% of each run, Pallas kernels for 31% -> 35%
where the time goes in v4:
time: 147 us; the launch traced here: 146 us
  Pallas kernels  50.5 us (34%)
  waiting for transfers between devices  32 us (22%)
  other arithmetic  19.2 us (13%)
  local copies, waits for them, and re-layouts  17.9 us (12%)
  between operations  13.5 us (9%)
  starting transfers between devices  13.2 us (9%)
    pallas_call x2, Pallas kernels, correlate(): pl.pallas_call(correlate_kernel, grid=(chunk_num,), in_specs=[whole(x.sha...  45.6 us
    reduce_scatter x2, waiting for transfers between devices, local(): stacked = lax.psum_scatter(partial, 'tm', scatter_dimension=0, tiled=True)  21.7 us
    convert_element_type x1, other arithmetic, make_table(): (-jnp.sin(angle) * scale).astype(jnp.bfloat16)  18.1 us
    all_to_all x2, starting transfers between devices, local(): lax.all_to_all(leaving, 'sta', split_axis=0, concat_axis=0, tiled=True)  7.96 us
    unnamed x6, local copies, waits for them, and re-layouts  6.08 us
    all_to_all x1, waiting for transfers between devices, local(): lax.all_to_all(copies, 'sta', split_axis=0, concat_axis=0, tiled=True)  6.06 us
    all_to_all x1, starting transfers between devices, local(): lax.all_to_all(copies, 'sta', split_axis=0, concat_axis=0, tiled=True)  5.17 us
    pallas_call x1, Pallas kernels, whiten_sources(): pl.pallas_call(sources_kernel, in_specs=[pl.BlockSpec(memory_space=pltpu....  4.9 us
  transfers between devices with their start and end apart: 5, of which 4 were waited for; matrix products, arithmetic and copies ran while one was open for 19% of the time, Pallas kernels for 35%

profile of v4, /device:TPU:0, one launch (start us, length us, event | category | flops | bytes accessed | tf_op | source)
XLA Modules:
  0.0 146.3 jit_solution(1910893003260439925)
XLA Ops:
  6.5 0.8 reshape.17
  7.3 3.0 %gather_fusion = bf16[24,2,2,512]{3,2,1,0:T(2,128)(2,1)S(1)} fusion(bf16[2,1024,2,512]{3,2,1,0:T(2,128)(2,1)} %param.2, s32[1024]{0:T(1024)S(1)} %pad_clamp_fusion), kind=kCustom, calls=%fused_computation | custom fusion | bytes 196704 | tf_op jit(solution)/shard_map/jit(_take)/gather | solution.py:175
  10.3 1.0 broadcast_in_dim.11
  11.3 5.2 %all-to-all-start.1 = ((bf16[8,2,2,24,512]{4,3,2,1,0:T(8,128)(2,1)}), bf16[8,2,2,24,512]{4,3,2,1,0:T(8,128)(2,1)S(1)}, u32[]{:S(2)}, u32[]{:S(2)}) async-start(bf16[8,2,2,24,512]{4,3,2,1,0:T(8,128)(2,1)} %broadcast_in_dim.11), calls=%async_computation.1 | async-start | bytes 1572864 | tf_op jit(solution)/shard_map/all_to_all | solution.py:177
  16.4 4.7 %fusion = (bf16[2,8,64,2,512]{4,3,2,1,0:T(2,128)(2,1)S(1)}, bf16[2,8,64,2,512]{4,3,2,1,0:T(2,128)(2,1)S(1)}) fusion(bf16[2,8,128,2,512]{4,3,2,1,0:T(2,128)(2,1)} %bitcast.10), kind=kLoop, calls=%fused_computation.11 | loop fusion | bytes 8388608 | tf_op jit(solution)/shard_map/slice | solution.py:184
  21.1 1.8 %copy.20 = bf16[2,8,64,2,512]{4,2,3,0,1:T(8,128)(2,1)} copy(bf16[2,8,64,2,512]{4,3,2,1,0:T(2,128)(2,1)S(1)} %get-tuple-element.15) | data formatting | bytes 4194304
  23.0 6.1 %all-to-all-done.1.y_ref = bf16[8,2,2,24,512]{4,3,2,1,0:T(8,128)(2,1)S(1)} async-done(((bf16[8,2,2,24,512]{4,3,2,1,0:T(8,128)(2,1)}), bf16[8,2,2,24,512]{4,3,2,1,0:T(8,128)(2,1)S(1)}, u32[]{:S(2)}, u32[]{:S(2)}) %all-to-all-start.1) | async-done | bytes 786464 | tf_op jit(solution)/shard_map/all_to_all | solution.py:177
  29.0 4.4 %all-to-all-start = ((bf16[8,2,2,64,512]{4,3,2,1,0:T(8,128)(2,1)}), bf16[8,2,2,64,512]{4,3,2,1,0:T(8,128)(2,1)}, u32[]{:S(2)}, u32[]{:S(2)}) async-start(bf16[8,2,2,64,512]{4,3,2,1,0:T(8,128)(2,1)} %bitcast.8), calls=%async_computation | async-start | bytes 4194304 | tf_op jit(solution)/shard_map/all_to_all | solution.py:188
  33.4 1.8 %copy.21 = bf16[2,8,64,2,512]{4,2,3,0,1:T(8,128)(2,1)} copy(bf16[2,8,64,2,512]{4,3,2,1,0:T(2,128)(2,1)S(1)} %get-tuple-element.16) | data formatting | bytes 4194304
  35.2 18.1 %multiply_convert_fusion = (bf16[8,512,256]{2,1,0:T(8,128)(2,1)}, bf16[8,512,256]{2,1,0:T(8,128)(2,1)}) fusion(s32[8]{0:T(128)S(1)} %iota_multiply_fusion, s32[256]{0:T(256)S(1)} %iota_add_fusion), kind=kLoop, calls=%fused_computation.1 | loop fusion | flops 10485760 | bytes 4195360 | tf_op jit(solution)/shard_map/convert_element_type | solution.py:30
  53.3 4.9 %shard_map.28.y_ref = f32[8,4,24,512]{3,2,1,0:T(8,128)S(1)} custom-call(bf16[8,2,2,24,512]{4,3,2,1,0:T(8,128)(2,1)S(1)} %all-to-all-done.1.y_ref), custom_call_target="tpu_custom_call" | custom-call | flops 400000000 | bytes 3145728 | tf_op jit(solution)/shard_map/pallas_call | solution.py:85
  58.2 1.1 copy-done
  59.4 0.7 all-to-all-done.x_ref
  60.0 3.6 %all-to-all-start.2 = ((bf16[8,2,2,64,512]{4,3,2,1,0:T(8,128)(2,1)}), bf16[8,2,2,64,512]{4,3,2,1,0:T(8,128)(2,1)S(1)}, u32[]{:S(2)}, u32[]{:S(2)}) async-start(bf16[8,2,2,64,512]{4,3,2,1,0:T(8,128)(2,1)} %bitcast.9), calls=%async_computation.3 | async-start | bytes 4194304 | tf_op jit(solution)/shard_map/all_to_all | solution.py:188
  63.6 0.0 reduce-scatter.3.cloned.1.call-start
  63.7 22.8 %shard_map.29 = bf16[256,1536]{1,0:T(8,128)(2,1)} custom-call(bf16[8,2,2,64,512]{4,3,2,1,0:T(8,128)(2,1)} %all-to-all-done.x_ref, f32[8,4,24,512]{3,2,1,0:T(8,128)} %copy-done, bf16[8,512,256]{2,1,0:T(8,128)(2,1)} %get-tuple-element.12.tr_ref, bf16[8,512,256]{2,1,0:T(8,128)(2,1)} %get-tuple-element.13.ti_ref), custom_call_target="tpu_custom_call" | custom-call | flops 12884901888 | bytes 12582912 | tf_op jit(solution)/shard_map/pallas_call | solution.py:141
  86.6 0.0 reduce-scatter.5.cloned.1.call-start
  86.6 3.6 %all-to-all-done.2.x_ref = bf16[8,2,2,64,512]{4,3,2,1,0:T(8,128)(2,1)S(1)} async-done(((bf16[8,2,2,64,512]{4,3,2,1,0:T(8,128)(2,1)}), bf16[8,2,2,64,512]{4,3,2,1,0:T(8,128)(2,1)S(1)}, u32[]{:S(2)}, u32[]{:S(2)}) %all-to-all-start.2) | async-done | bytes 2097184 | tf_op jit(solution)/shard_map/all_to_all | solution.py:188
  90.2 1.3 copy-done.1
  91.6 22.8 %shard_map.30 = bf16[256,1536]{1,0:T(8,128)(2,1)} custom-call(bf16[8,2,2,64,512]{4,3,2,1,0:T(8,128)(2,1)} %copy-done.1, f32[8,4,24,512]{3,2,1,0:T(8,128)} %copy-done, bf16[8,512,256]{2,1,0:T(8,128)(2,1)} %get-tuple-element.12.tr_ref, bf16[8,512,256]{2,1,0:T(8,128)(2,1)} %get-tuple-element.13.ti_ref), custom_call_target="tpu_custom_call" | custom-call | flops 12884901888 | bytes 12582912 | tf_op jit(solution)/shard_map/pallas_call | solution.py:141
  114.4 1.2 reshape.13
  115.6 21.6 %reduce-scatter.5.cloned.1.call-done = bf16[64,1536]{1,0:T(8,128)(2,1)} async-done(((bf16[256,1536]{1,0:T(8,128)(2,1)}), bf16[64,1536]{1,0:T(8,128)(2,1)}) %reduce-scatter.5.cloned.1.call-update) | async-done | bytes 196624 | tf_op jit(solution)/shard_map/reduce_scatter | solution.py:192
  137.2 1.2 reshape.14
  138.4 1.1 convert_bitcast_fusion
  (9 shorter events, 0.1 us)
Async XLA Ops:
  11.3 17.8 %all-to-all-start.1 = ((bf16[8,2,2,24,512]{4,3,2,1,0:T(8,128)(2,1)}), bf16[8,2,2,24,512]{4,3,2,1,0:T(8,128)(2,1)S(1)}, u32[]{:S(2)}, u32[]{:S(2)}) async-start(bf16[8,2,2,24,512]{4,3,2,1,0:T(8,128)(2,1)} %broadcast_in_dim.11), calls=%async_computation.1 | async-start | bytes 1572864 | tf_op jit(solution)/shard_map/all_to_all | solution.py:177
  29.0 31.0 %all-to-all-start = ((bf16[8,2,2,64,512]{4,3,2,1,0:T(8,128)(2,1)}), bf16[8,2,2,64,512]{4,3,2,1,0:T(8,128)(2,1)}, u32[]{:S(2)}, u32[]{:S(2)}) async-start(bf16[8,2,2,64,512]{4,3,2,1,0:T(8,128)(2,1)} %bitcast.8), calls=%async_computation | async-start | bytes 4194304 | tf_op jit(solution)/shard_map/all_to_all | solution.py:188
  58.2 1.2 copy-start
  60.0 30.2 %all-to-all-start.2 = ((bf16[8,2,2,64,512]{4,3,2,1,0:T(8,128)(2,1)}), bf16[8,2,2,64,512]{4,3,2,1,0:T(8,128)(2,1)S(1)}, u32[]{:S(2)}, u32[]{:S(2)}) async-start(bf16[8,2,2,64,512]{4,3,2,1,0:T(8,128)(2,1)} %bitcast.9), calls=%async_computation.3 | async-start | bytes 4194304 | tf_op jit(solution)/shard_map/all_to_all | solution.py:188
  63.6 50.7 %reduce-scatter.3.cloned.1.call-start = ((), (), s32[]{:S(2)}) async-start(), calls=%async_computation.5 | async-start | bytes 983040 | tf_op jit(solution)/shard_map/reduce_scatter | solution.py:192
  86.6 50.6 %reduce-scatter.5.cloned.1.call-start = ((), (), s32[]{:S(2)}) async-start(), calls=%async_computation.6 | async-start | bytes 983040 | tf_op jit(solution)/shard_map/reduce_scatter | solution.py:192
  90.2 1.3 copy-start.1
Sparse Core Ops, SparseCore 0:
  86.7 24.9 reduce-scatter.2
  114.5 22.6 reduce-scatter.4

commit v5 on v4

--- a/solution.py
+++ b/solution.py
@@ -55,7 +55,7 @@
         near = twice(jnp.where((away >= -1) & (away <= 1), 1.0, 0.0))
         return total + jnp.dot(jnp.concatenate(terms, axis=0), near, preferred_element_type=jnp.float32)
 
-    total = lax.fori_loop(0, chunk_num, add_chunk, jnp.zeros((hours * rows, COLS), jnp.float32))
+    total = lax.fori_loop(0, chunk_num, add_chunk, jnp.zeros((hours * rows, COLS), jnp.float32), unroll=4)
     inv_ref[...] = split_wide(1.0 / (total / (3.0 * BLOCK) + EPSILON))
 
 
@@ -93,9 +93,11 @@
     )(y)
 
 
-def correlate_kernel(x_ref, y_ref, tr_ref, ti_ref, o_ref, inv_x, xw, real_a, imag_a, real_b, imag_b, total):
+def correlate_kernel(x_ref, y_ref, tr_ref, ti_ref, o_ref, inv_x, xw, *buffers):
     chunk = pl.program_id(0)
     chunk_num, hours, _, rows, width = x_ref.shape
+    total = buffers[-1]
+    crosses = [buffers[2 * step:2 * step + 2] for step in range(ROUNDS)]
 
     @pl.when(chunk == 0)
     def _():
@@ -108,8 +110,14 @@
             piece = x_ref[chunk, hour, part].astype(jnp.float32) * scale[hour * rows:(hour + 1) * rows]
             xw[hour * 2 + part] = piece.astype(jnp.bfloat16)
 
+    def project(step):
+        real_ref, imag_ref = crosses[step]
+        total[step] += jnp.dot(real_ref[...], tr_ref[0], preferred_element_type=jnp.float32) + jnp.dot(
+            imag_ref[...], ti_ref[0], preferred_element_type=jnp.float32
+        )
+
     for step in range(ROUNDS):
-        real_ref, imag_ref = ((real_a, imag_a), (real_b, imag_b))[step % 2]
+        real_ref, imag_ref = crosses[step]
         for k in range(NSRC):
             for low in range(0, width, 128):
                 lanes = slice(low, low + 128)
@@ -123,9 +131,9 @@
                 imag = (y[1] * x[0] - y[0] * x[1]) + (y[3] * x[2] - y[2] * x[3])
                 real_ref[k * rows:(k + 1) * rows, lanes] = real.reshape(rows, 128)
                 imag_ref[k * rows:(k + 1) * rows, lanes] = imag.reshape(rows, 128)
-        total[step] += jnp.dot(real_ref[...], tr_ref[0], preferred_element_type=jnp.float32) + jnp.dot(
-            imag_ref[...], ti_ref[0], preferred_element_type=jnp.float32
-        )
+        if step:
+            project(step - 1)
+    project(ROUNDS - 1)
 
     @pl.when(chunk == chunk_num - 1)
     def _():
@@ -152,10 +160,7 @@
         scratch_shapes=[
             pltpu.VMEM((hours * rows, 2 * COLS), jnp.bfloat16),
             pltpu.VMEM((hours * 2, rows, width), jnp.bfloat16),
-            cross,
-            cross,
-            cross,
-            cross,
+            *([cross] * (2 * ROUNDS)),
             pltpu.VMEM((ROUNDS, NSRC * rows, LAGS), jnp.float32),
         ],
         compiler_params=pltpu.CompilerParams(

time: 147 us -> 146 us (level)
  Pallas kernels: 50.5 us -> 48.2 us
    pallas_call x2, Pallas kernels: 45.6 us -> 44 us  [correlate(): pl.pallas_call(correlate_kernel, grid=(chunk_num,), in_specs=[whole(x.sha...]
  transfers between devices with their start and end apart: 5 -> 5, of which waited for: 4 -> 4; matrix products, arithmetic and copies ran while one was open for 19% -> 19% of each run, Pallas kernels for 35% -> 33%
where the time goes in v5:
time: 146 us
  Pallas kernels  48.2 us (33%)
  waiting for transfers between devices  33.4 us (23%)
  other arithmetic  19.2 us (13%)
  local copies, waits for them, and re-layouts  17.9 us (12%)
  between operations  13.5 us (9%)
  starting transfers between devices  13.4 us (9%)
    pallas_call x2, Pallas kernels, correlate(): pl.pallas_call(correlate_kernel, grid=(chunk_num,), in_specs=[whole(x.sha...  44 us
    reduce_scatter x2, waiting for transfers between devices, local(): stacked = lax.psum_scatter(partial, 'tm', scatter_dimension=0, tiled=True)  21.7 us
    convert_element_type x1, other arithmetic, make_table(): (-jnp.sin(angle) * scale).astype(jnp.bfloat16)  18.1 us
    all_to_all x2, starting transfers between devices, local(): lax.all_to_all(leaving, 'sta', split_axis=0, concat_axis=0, tiled=True)  7.96 us
    unnamed x6, local copies, waits for them, and re-layouts  6.08 us
    all_to_all x1, waiting for transfers between devices, local(): lax.all_to_all(copies, 'sta', split_axis=0, concat_axis=0, tiled=True)  6.06 us
    all_to_all x2, waiting for transfers between devices, local(): lax.all_to_all(leaving, 'sta', split_axis=0, concat_axis=0, tiled=True)  5.66 us
    all_to_all x1, starting transfers between devices, local(): lax.all_to_all(copies, 'sta', split_axis=0, concat_axis=0, tiled=True)  5.17 us
  transfers between devices with their start and end apart: 5, of which 4 were waited for; matrix products, arithmetic and copies ran while one was open for 19% of the time, Pallas kernels for 33%

profile of v5, /device:TPU:0, one launch (start us, length us, event | category | flops | bytes accessed | tf_op | source)
XLA Modules:
  0.0 145.5 jit_solution(12910483584179314323)
XLA Ops:
  6.5 0.8 reshape.17
  7.3 2.9 %gather_fusion = bf16[24,2,2,512]{3,2,1,0:T(2,128)(2,1)S(1)} fusion(bf16[2,1024,2,512]{3,2,1,0:T(2,128)(2,1)} %param.2, s32[1024]{0:T(1024)S(1)} %pad_clamp_fusion), kind=kCustom, calls=%fused_computation | custom fusion | bytes 196704 | tf_op jit(solution)/shard_map/jit(_take)/gather | solution.py:180
  10.3 1.0 broadcast_in_dim.11
  11.3 5.2 %all-to-all-start.1 = ((bf16[8,2,2,24,512]{4,3,2,1,0:T(8,128)(2,1)}), bf16[8,2,2,24,512]{4,3,2,1,0:T(8,128)(2,1)S(1)}, u32[]{:S(2)}, u32[]{:S(2)}) async-start(bf16[8,2,2,24,512]{4,3,2,1,0:T(8,128)(2,1)} %broadcast_in_dim.11), calls=%async_computation.1 | async-start | bytes 1572864 | tf_op jit(solution)/shard_map/all_to_all | solution.py:182
  16.4 4.7 %fusion = (bf16[2,8,64,2,512]{4,3,2,1,0:T(2,128)(2,1)S(1)}, bf16[2,8,64,2,512]{4,3,2,1,0:T(2,128)(2,1)S(1)}) fusion(bf16[2,8,128,2,512]{4,3,2,1,0:T(2,128)(2,1)} %bitcast.10), kind=kLoop, calls=%fused_computation.11 | loop fusion | bytes 8388608 | tf_op jit(solution)/shard_map/slice | solution.py:189
  21.1 1.8 %copy.20 = bf16[2,8,64,2,512]{4,2,3,0,1:T(8,128)(2,1)} copy(bf16[2,8,64,2,512]{4,3,2,1,0:T(2,128)(2,1)S(1)} %get-tuple-element.15) | data formatting | bytes 4194304
  23.0 6.1 %all-to-all-done.1.y_ref = bf16[8,2,2,24,512]{4,3,2,1,0:T(8,128)(2,1)S(1)} async-done(((bf16[8,2,2,24,512]{4,3,2,1,0:T(8,128)(2,1)}), bf16[8,2,2,24,512]{4,3,2,1,0:T(8,128)(2,1)S(1)}, u32[]{:S(2)}, u32[]{:S(2)}) %all-to-all-start.1) | async-done | bytes 786464 | tf_op jit(solution)/shard_map/all_to_all | solution.py:182
  29.0 4.4 %all-to-all-start = ((bf16[8,2,2,64,512]{4,3,2,1,0:T(8,128)(2,1)}), bf16[8,2,2,64,512]{4,3,2,1,0:T(8,128)(2,1)}, u32[]{:S(2)}, u32[]{:S(2)}) async-start(bf16[8,2,2,64,512]{4,3,2,1,0:T(8,128)(2,1)} %bitcast.8), calls=%async_computation | async-start | bytes 4194304 | tf_op jit(solution)/shard_map/all_to_all | solution.py:193
  33.4 1.8 %copy.21 = bf16[2,8,64,2,512]{4,2,3,0,1:T(8,128)(2,1)} copy(bf16[2,8,64,2,512]{4,3,2,1,0:T(2,128)(2,1)S(1)} %get-tuple-element.16) | data formatting | bytes 4194304
  35.2 18.1 %multiply_convert_fusion = (bf16[8,512,256]{2,1,0:T(8,128)(2,1)}, bf16[8,512,256]{2,1,0:T(8,128)(2,1)}) fusion(s32[8]{0:T(128)S(1)} %iota_multiply_fusion, s32[256]{0:T(256)S(1)} %iota_add_fusion), kind=kLoop, calls=%fused_computation.1 | loop fusion | flops 10485760 | bytes 4195360 | tf_op jit(solution)/shard_map/convert_element_type | solution.py:30
  53.3 4.1 %shard_map.28.y_ref = f32[8,4,24,512]{3,2,1,0:T(8,128)S(1)} custom-call(bf16[8,2,2,24,512]{4,3,2,1,0:T(8,128)(2,1)S(1)} %all-to-all-done.1.y_ref), custom_call_target="tpu_custom_call" | custom-call | flops 400000000 | bytes 3145728 | tf_op jit(solution)/shard_map/pallas_call | solution.py:85
  57.5 1.1 copy-done
  58.6 1.4 all-to-all-done.x_ref
  60.0 3.6 %all-to-all-start.2 = ((bf16[8,2,2,64,512]{4,3,2,1,0:T(8,128)(2,1)}), bf16[8,2,2,64,512]{4,3,2,1,0:T(8,128)(2,1)S(1)}, u32[]{:S(2)}, u32[]{:S(2)}) async-start(bf16[8,2,2,64,512]{4,3,2,1,0:T(8,128)(2,1)} %bitcast.9), calls=%async_computation.3 | async-start | bytes 4194304 | tf_op jit(solution)/shard_map/all_to_all | solution.py:193
  63.6 0.0 reduce-scatter.3.cloned.1.call-start
  63.7 22.1 %shard_map.29 = bf16[256,1536]{1,0:T(8,128)(2,1)} custom-call(bf16[8,2,2,64,512]{4,3,2,1,0:T(8,128)(2,1)} %all-to-all-done.x_ref, f32[8,4,24,512]{3,2,1,0:T(8,128)} %copy-done, bf16[8,512,256]{2,1,0:T(8,128)(2,1)} %get-tuple-element.12.tr_ref, bf16[8,512,256]{2,1,0:T(8,128)(2,1)} %get-tuple-element.13.ti_ref), custom_call_target="tpu_custom_call" | custom-call | flops 12884901888 | bytes 12582912 | tf_op jit(solution)/shard_map/pallas_call | solution.py:149
  85.8 0.2 reduce-scatter.5.cloned.1.call-start
  86.0 4.2 %all-to-all-done.2.x_ref = bf16[8,2,2,64,512]{4,3,2,1,0:T(8,128)(2,1)S(1)} async-done(((bf16[8,2,2,64,512]{4,3,2,1,0:T(8,128)(2,1)}), bf16[8,2,2,64,512]{4,3,2,1,0:T(8,128)(2,1)S(1)}, u32[]{:S(2)}, u32[]{:S(2)}) %all-to-all-start.2) | async-done | bytes 2097184 | tf_op jit(solution)/shard_map/all_to_all | solution.py:193
  90.2 1.3 copy-done.1
  91.6 22.0 %shard_map.30 = bf16[256,1536]{1,0:T(8,128)(2,1)} custom-call(bf16[8,2,2,64,512]{4,3,2,1,0:T(8,128)(2,1)} %copy-done.1, f32[8,4,24,512]{3,2,1,0:T(8,128)} %copy-done, bf16[8,512,256]{2,1,0:T(8,128)(2,1)} %get-tuple-element.12.tr_ref, bf16[8,512,256]{2,1,0:T(8,128)(2,1)} %get-tuple-element.13.ti_ref), custom_call_target="tpu_custom_call" | custom-call | flops 12884901888 | bytes 12582912 | tf_op jit(solution)/shard_map/pallas_call | solution.py:149
  113.6 1.2 reshape.13
  114.8 21.6 %reduce-scatter.5.cloned.1.call-done = bf16[64,1536]{1,0:T(8,128)(2,1)} async-done(((bf16[256,1536]{1,0:T(8,128)(2,1)}), bf16[64,1536]{1,0:T(8,128)(2,1)}) %reduce-scatter.5.cloned.1.call-update) | async-done | bytes 196624 | tf_op jit(solution)/shard_map/reduce_scatter | solution.py:197
  136.4 1.2 reshape.14
  137.6 1.1 convert_bitcast_fusion
  (9 shorter events, 0.1 us)
Async XLA Ops:
  11.3 17.8 %all-to-all-start.1 = ((bf16[8,2,2,24,512]{4,3,2,1,0:T(8,128)(2,1)}), bf16[8,2,2,24,512]{4,3,2,1,0:T(8,128)(2,1)S(1)}, u32[]{:S(2)}, u32[]{:S(2)}) async-start(bf16[8,2,2,24,512]{4,3,2,1,0:T(8,128)(2,1)} %broadcast_in_dim.11), calls=%async_computation.1 | async-start | bytes 1572864 | tf_op jit(solution)/shard_map/all_to_all | solution.py:182
  29.0 31.0 %all-to-all-start = ((bf16[8,2,2,64,512]{4,3,2,1,0:T(8,128)(2,1)}), bf16[8,2,2,64,512]{4,3,2,1,0:T(8,128)(2,1)}, u32[]{:S(2)}, u32[]{:S(2)}) async-start(bf16[8,2,2,64,512]{4,3,2,1,0:T(8,128)(2,1)} %bitcast.8), calls=%async_computation | async-start | bytes 4194304 | tf_op jit(solution)/shard_map/all_to_all | solution.py:193
  57.4 1.2 copy-start
  60.0 30.2 %all-to-all-start.2 = ((bf16[8,2,2,64,512]{4,3,2,1,0:T(8,128)(2,1)}), bf16[8,2,2,64,512]{4,3,2,1,0:T(8,128)(2,1)S(1)}, u32[]{:S(2)}, u32[]{:S(2)}) async-start(bf16[8,2,2,64,512]{4,3,2,1,0:T(8,128)(2,1)} %bitcast.9), calls=%async_computation.3 | async-start | bytes 4194304 | tf_op jit(solution)/shard_map/all_to_all | solution.py:193
  63.6 49.9 %reduce-scatter.3.cloned.1.call-start = ((), (), s32[]{:S(2)}) async-start(), calls=%async_computation.5 | async-start | bytes 983040 | tf_op jit(solution)/shard_map/reduce_scatter | solution.py:197
  85.8 50.6 %reduce-scatter.5.cloned.1.call-start = ((), (), s32[]{:S(2)}) async-start(), calls=%async_computation.6 | async-start | bytes 983040 | tf_op jit(solution)/shard_map/reduce_scatter | solution.py:197
  90.2 1.3 copy-start.1
Sparse Core Ops, SparseCore 0:
  85.9 24.9 reduce-scatter.2
  113.7 22.6 reduce-scatter.4
